TPU v7x, 512 devices: a whole 4x4x16 slice. The times are simulated.
512 devices in a mesh: gx: 16 (over z), gy: 8 (over y, core), gz: 4 (over x).
Axes of the slice: x: 4, y: 4, z: 16, core: 2. Of those that a mesh axis runs over, the one named last changes fastest.
Arguments:
- right_side: float32 [256, 128, 512], P('gx', 'gy', 'gz'), may hold values from -6 to 6
- conductivity: float32 [256, 128, 512], P('gx', 'gy', 'gz'), may hold values from 0.2 to 5
Outputs:
- solution_field: float32 [256, 128, 512], P('gx', 'gy', 'gz')
All inputs are finite; a program needn't handle non-finite values.
Results may differ from a plain program's by a relative error of at most 0.00012.
Values sent between devices are 32-bit elements; how exact they have to be, the bound alone decides.
A program may use at most 128 MiB of HBM per device.

v0:
```python
import jax
import jax.numpy as jnp
from jax import lax
from jax.sharding import PartitionSpec as P

LEVELS = 4
CG_ITERS = 8


THETA = 1.125
DELTA = 0.875


def padded_2(block, sides, width):
    for axis, dim in sides:
        count = lax.axis_size(axis)
        forward = [(i, i + 1) for i in range(count - 1)]
        backward = [(target, source) for source, target in forward]
        low = lax.ppermute(
            lax.slice_in_dim(block, block.shape[dim] - width, None, axis=dim), axis, forward
        )
        high = lax.ppermute(lax.slice_in_dim(block, 0, width, axis=dim), axis, backward)
        block = jnp.concatenate([low, block, high], axis=dim)
    return block


def cheb_table():
    sigma = THETA / DELTA
    rho_now = 1.0 / sigma
    table = []
    for sweep in range(3):
        rho_next = 1.0 / (2.0 * sigma - rho_now)
        table.append((rho_next * rho_now, 2.0 * rho_next / DELTA))
        rho_now = rho_next
    return table


def shifted(padded):
    return [
        padded[2:, 1:-1, 1:-1],
        padded[:-2, 1:-1, 1:-1],
        padded[1:-1, 2:, 1:-1],
        padded[1:-1, :-2, 1:-1],
        padded[1:-1, 1:-1, 2:],
        padded[1:-1, 1:-1, :-2],
    ]


def total_of(terms):
    running = terms[0]
    for other in terms[1:]:
        running = running + other
    return running


def face_weights(coef_pad, scale):
    centre = coef_pad[1:-1, 1:-1, 1:-1]
    return [0.5 * scale * (centre + other) for other in shifted(coef_pad)]


def operate(padded, weights, diagonal):
    return diagonal * padded[1:-1, 1:-1, 1:-1] - total_of(
        [w_face * near for w_face, near in zip(weights, shifted(padded))]
    )


def coarsen(field):
    size_a, size_b, size_c = field.shape
    return jnp.mean(field.reshape(size_a // 2, 2, size_b // 2, 2, size_c // 2, 2), axis=(1, 3, 5))


def refine(field):
    size_a, size_b, size_c = field.shape
    spread = jnp.broadcast_to(field[:, None, :, None, :, None], (size_a, 2, size_b, 2, size_c, 2))
    return spread.reshape(2 * size_a, 2 * size_b, 2 * size_c)


def rim(field):
    return padded_2(field, (("gx", 0), ("gy", 1), ("gz", 2)), 1)


def plain_parts(conductivity, scale):
    coef_pad = padded_2(conductivity, (("gx", 0), ("gy", 1), ("gz", 2)), 1)
    weights = face_weights(coef_pad, scale)
    diagonal = total_of(weights)
    return (weights, diagonal, 1.0 / diagonal)


def presmooth(source, parts):
    weights, diagonal, inverse = parts
    table = cheb_table()
    solution = jnp.zeros_like(source)
    residual = source
    step_dir = inverse * residual / THETA
    for sweep in range(4):
        solution = solution + step_dir
        residual = residual - operate(rim(step_dir), weights, diagonal)
        if sweep < 3:
            step_dir = table[sweep][0] * step_dir + table[sweep][1] * (inverse * residual)
    return (solution, residual)


def postsmooth(source, solution, parts):
    weights, diagonal, inverse = parts
    table = cheb_table()
    residual = source - operate(rim(solution), weights, diagonal)
    step_dir = inverse * residual / THETA
    for sweep in range(4):
        solution = solution + step_dir
        if sweep < 3:
            residual = residual - operate(rim(step_dir), weights, diagonal)
            step_dir = table[sweep][0] * step_dir + table[sweep][1] * (inverse * residual)
    return solution


def plain_start(source, conductivity, scale):
    parts = plain_parts(conductivity, scale)
    solution, residual = presmooth(source, parts)
    return (solution, residual, parts)


def assemble(flat, brick):
    count_x, count_y, count_z = (lax.axis_size("gx"), lax.axis_size("gy"), lax.axis_size("gz"))
    blocks = flat.reshape(count_x, count_y, count_z, brick[0], brick[1], brick[2])
    blocks = blocks.transpose(0, 3, 1, 4, 2, 5)
    return blocks.reshape(count_x * brick[0], count_y * brick[1], count_z * brick[2])


def bottom_everywhere(source, conductivity, scale):
    brick = source.shape
    flat_source, flat_coef = (
        lax.all_gather(source.reshape(1, -1), ("gx", "gy", "gz"), axis=0, tiled=True),
        lax.all_gather(conductivity.reshape(1, -1), ("gx", "gy", "gz"), axis=0, tiled=True),
    )
    whole_source = assemble(flat_source, brick)
    whole_coef = assemble(flat_coef, brick)
    weights = face_weights(jnp.pad(whole_coef, 1), scale)
    diagonal = total_of(weights)
    solution = jnp.zeros_like(whole_source)
    residual = whole_source
    direction = whole_source
    norm_now = jnp.sum(residual * residual)
    for sweep in range(CG_ITERS):
        image = operate(jnp.pad(direction, 1), weights, diagonal)
        alpha = norm_now / jnp.sum(direction * image)
        solution = solution + alpha * direction
        residual = residual - alpha * image
        norm_next = jnp.sum(residual * residual)
        direction = residual + norm_next / norm_now * direction
        norm_now = norm_next
    starts = (
        lax.axis_index("gx") * brick[0],
        lax.axis_index("gy") * brick[1],
        lax.axis_index("gz") * brick[2],
    )
    return lax.dynamic_slice(solution, starts, brick)


def cycle(source, conductivity, level):
    scale = 0.25**level
    if level == LEVELS:
        return bottom_everywhere(source, conductivity, scale)
    solution, residual, parts = plain_start(source, conductivity, scale)
    correction = cycle(coarsen(residual), coarsen(conductivity), level + 1)
    solution = solution + refine(correction)
    return postsmooth(source, solution, parts)


def local(right_side, conductivity):
    return cycle(right_side, conductivity, 0)


def solution(mesh):
    in_specs = (P("gx", "gy", "gz"), P("gx", "gy", "gz"))
    out_specs = P("gx", "gy", "gz")
    return jax.shard_map(local, mesh=mesh, in_specs=in_specs, out_specs=out_specs, check_vma=False)
```

profile of v0, /device:TPU:1, one launch (start us, length us, event | category | flops | bytes accessed | tf_op | source)
XLA Modules:
  0.0 1010.8 jit_solution(3037965828782282874)
XLA Ops:
  9.7 6.7 collective-permute-start.2
  45.6 4.7 collective-permute-start.11
  71.2 4.7 collective-permute-start.17
  83.3 5.9 collective-permute-start.19
  89.2 9.8 reshape.70
  116.8 5.5 collective-permute-start.25
  123.9 5.8 collective-permute-start.31
  131.8 4.9 collective-permute-start.27
  154.8 9.8 reshape.71
  170.0 5.8 collective-permute-start.37
  178.7 5.4 collective-permute-start.39
  193.4 5.5 collective-permute-start.43
  201.6 5.9 collective-permute-start.45
  217.2 5.5 collective-permute-start.49
  225.4 5.9 collective-permute-start.51
  239.4 5.5 collective-permute-start.55
  246.5 5.7 collective-permute-start.61
  254.2 5.0 collective-permute-start.57
  280.0 5.7 collective-permute-start.67
  288.7 5.4 collective-permute-start.69
  295.4 5.7 collective-permute-start.85
  309.5 5.5 collective-permute-start.73
  331.1 5.5 collective-permute-start.79
  339.2 5.9 collective-permute-start.81
  358.4 5.7 collective-permute-start.91
  373.3 4.9 collective-permute-start.95
  384.0 5.5 collective-permute-start.97
  405.8 5.7 collective-permute-start.103
  414.3 5.8 collective-permute-start.105
  428.9 5.7 collective-permute-start.109
  437.3 5.9 collective-permute-start.111
  452.1 5.5 collective-permute-start.115
  460.2 5.9 collective-permute-start.117
  473.9 116.2 %all-reduce.11 = (f32[4096]{0:T(1024)S(1)}, f32[4096]{0:T(1024)S(1)}) all-reduce(f32[4096]{0:T(1024)S(1)} %multiply_dynamic-update-slice_fusion, f32[4096]{0:T(1024)S(1)} %multiply_dynamic-update-slice_fusion.1), channel_id=3, replica_groups=mesh['gx'=16,'gy'=8,'gz'=4] {'gx','gy','gz'}, use_global_device_ids=true, to_apply=%add.10 | all-reduce | flops 8192 | bytes 65536
  671.7 5.7 collective-permute-start.135
  693.4 5.9 collective-permute-start.141
  715.5 5.9 collective-permute-start.147
  730.4 4.7 collective-permute-start.151
  737.7 5.9 collective-permute-start.153
  752.7 5.7 collective-permute-start.157
  761.1 5.9 collective-permute-start.159
  776.0 5.7 collective-permute-start.163
  784.4 6.1 collective-permute-start.165
  800.2 5.7 collective-permute-start.169
  808.6 5.9 collective-permute-start.171
  824.1 5.7 collective-permute-start.175
  832.6 5.9 collective-permute-start.177
  848.2 5.7 collective-permute-start.181
  856.6 5.9 collective-permute-start.183
  872.2 5.7 collective-permute-start.187
  880.6 5.9 collective-permute-start.189
  898.8 6.9 reshape.76
  907.1 5.7 collective-permute-start.193
  915.6 5.9 collective-permute-start.195
  923.7 4.6 collective-permute-start.197
  932.8 5.7 collective-permute-start.199
  941.2 5.9 collective-permute-start.201
  949.4 4.7 collective-permute-start.203
  958.6 5.7 collective-permute-start.205
  967.0 7.1 collective-permute-start.207
  976.3 4.7 collective-permute-start.209
  985.5 5.7 collective-permute-start.211
  994.0 5.9 collective-permute-start.213
  1002.2 4.7 collective-permute-start.215
  (626 shorter events, 507.3 us)
Async XLA Ops:
  9.7 8.6 collective-permute-start.2
  19.7 8.8 collective-permute-start.4
  21.0 8.3 collective-permute-start.5
  44.3 9.8 collective-permute-start.10
  45.6 9.4 collective-permute-start.11
  69.9 9.8 collective-permute-start.16
  71.2 9.4 collective-permute-start.17
  82.0 21.0 %collective-permute-start.18 = (f32[1,16,128]{2,1,0:T(8,128)S(1)}, f32[1,16,128]{2,1,0:T(8,128)S(1)}, u32[]{:S(2)}, u32[]{:S(2)}) collective-permute-start(f32[1,16,128]{2,1,0:T(8,128)S(1)} %get-tuple-element.158), channel_id=1, source_target_pairs={{32,0},{64,32},{96,64},{128,96},{160,128},{192,160},{224,192},{256... | collective-permute-start | bytes 24584 | tf_op jit(solution)/shard_map/ppermute | solution.py:22
  83.3 19.7 %collective-permute-start.19 = (f32[1,16,128]{2,1,0:T(8,128)S(1)}, f32[1,16,128]{2,1,0:T(8,128)S(1)}, u32[]{:S(2)}, u32[]{:S(2)}) collective-permute-start(f32[1,16,128]{2,1,0:T(8,128)S(1)} %get-tuple-element.157), channel_id=1, source_target_pairs={{0,32},{32,64},{64,96},{96,128},{128,160},{160,192},{192,224},{224... | collective-permute-start | bytes 24584 | tf_op jit(solution)/shard_map/ppermute | solution.py:19
  109.6 12.7 %collective-permute-start.22 = (f32[18,18,1]{2,1,0:T(8,128)S(1)}, f32[18,18,1]{2,1,0:T(8,128)S(1)}, u32[]{:S(2)}, u32[]{:S(2)}) collective-permute-start(f32[18,18,1]{2,1,0:T(8,128)S(1)} %get-tuple-element.121), channel_id=1, source_target_pairs={{1,0},{2,1},{3,2},{5,4},{6,5},{7,6},{9,8},{10,9},{11,10},{13,12},{... | collective-permute-start | bytes 3896 | tf_op jit(solution)/shard_map/ppermute | solution.py:22
  110.9 11.4 %collective-permute-start.23 = (f32[18,18,1]{2,1,0:T(8,128)S(1)}, f32[18,18,1]{2,1,0:T(8,128)S(1)}, u32[]{:S(2)}, u32[]{:S(2)}) collective-permute-start(f32[18,18,1]{2,1,0:T(8,128)S(1)} %get-tuple-element.122), channel_id=1, source_target_pairs={{0,1},{1,2},{2,3},{4,5},{5,6},{6,7},{8,9},{9,10},{10,11},{12,13},{... | collective-permute-start | bytes 3896 | tf_op jit(solution)/shard_map/ppermute | solution.py:19
  115.5 14.2 %collective-permute-start.24 = (f32[1,8,64]{2,1,0:T(8,128)S(1)}, f32[1,8,64]{2,1,0:T(8,128)S(1)}, u32[]{:S(2)}, u32[]{:S(2)}) collective-permute-start(f32[1,8,64]{2,1,0:T(8,128)S(1)} %get-tuple-element.220), channel_id=1, source_target_pairs={{32,0},{64,32},{96,64},{128,96},{160,128},{192,160},{224,192},{256... | collective-permute-start | bytes 6152 | tf_op jit(solution)/shard_map/ppermute | solution.py:22
  116.8 12.9 %collective-permute-start.25 = (f32[1,8,64]{2,1,0:T(8,128)S(1)}, f32[1,8,64]{2,1,0:T(8,128)S(1)}, u32[]{:S(2)}, u32[]{:S(2)}) collective-permute-start(f32[1,8,64]{2,1,0:T(8,128)S(1)} %get-tuple-element.221), channel_id=1, source_target_pairs={{0,32},{32,64},{64,96},{96,128},{128,160},{160,192},{192,224},{224... | collective-permute-start | bytes 6152 | tf_op jit(solution)/shard_map/ppermute | solution.py:19
  122.6 14.1 %collective-permute-start.30 = (f32[1,16,128]{2,1,0:T(8,128)S(1)}, f32[1,16,128]{2,1,0:T(8,128)S(1)}, u32[]{:S(2)}, u32[]{:S(2)}) collective-permute-start(f32[1,16,128]{2,1,0:T(8,128)S(1)} %get-tuple-element.156), channel_id=1, source_target_pairs={{32,0},{64,32},{96,64},{128,96},{160,128},{192,160},{224,192},{256... | collective-permute-start | bytes 24584 | tf_op jit(solution)/shard_map/ppermute | solution.py:22
  123.9 12.8 %collective-permute-start.31 = (f32[1,16,128]{2,1,0:T(8,128)S(1)}, f32[1,16,128]{2,1,0:T(8,128)S(1)}, u32[]{:S(2)}, u32[]{:S(2)}) collective-permute-start(f32[1,16,128]{2,1,0:T(8,128)S(1)} %get-tuple-element.155), channel_id=1, source_target_pairs={{0,32},{32,64},{64,96},{96,128},{128,160},{160,192},{192,224},{224... | collective-permute-start | bytes 24584 | tf_op jit(solution)/shard_map/ppermute | solution.py:19
  129.7 12.6 %collective-permute-start.26 = (f32[10,1,64]{2,1,0:T(1,128)S(1)}, f32[10,1,64]{2,1,0:T(1,128)S(1)}, u32[]{:S(2)}, u32[]{:S(2)}) collective-permute-start(f32[10,1,64]{2,1,0:T(1,128)S(1)} %get-tuple-element.203), channel_id=1, source_target_pairs={{4,0},{8,4},{12,8},{16,12},{20,16},{24,20},{28,24},{5,1},{9,5},{13... | collective-permute-start | bytes 7688 | tf_op jit(solution)/shard_map/ppermute | solution.py:22
  131.8 10.6 %collective-permute-start.27 = (f32[10,1,64]{2,1,0:T(1,128)S(1)}, f32[10,1,64]{2,1,0:T(1,128)S(1)}, u32[]{:S(2)}, u32[]{:S(2)}) collective-permute-start(f32[10,1,64]{2,1,0:T(1,128)S(1)} %get-tuple-element.202), channel_id=1, source_target_pairs={{0,4},{4,8},{8,12},{12,16},{16,20},{20,24},{24,28},{1,5},{5,9},{9,... | collective-permute-start | bytes 7688 | tf_op jit(solution)/shard_map/ppermute | solution.py:19
  143.3 11.3 %collective-permute-start.34 = (f32[18,18,1]{2,1,0:T(8,128)S(1)}, f32[18,18,1]{2,1,0:T(8,128)S(1)}, u32[]{:S(2)}, u32[]{:S(2)}) collective-permute-start(f32[18,18,1]{2,1,0:T(8,128)S(1)} %get-tuple-element.119), channel_id=1, source_target_pairs={{1,0},{2,1},{3,2},{5,4},{6,5},{7,6},{9,8},{10,9},{11,10},{13,12},{... | collective-permute-start | bytes 3896 | tf_op jit(solution)/shard_map/ppermute | solution.py:22
  144.6 10.0 collective-permute-start.35
  149.0 19.6 %collective-permute-start.28 = (f32[10,10,1]{2,1,0:T(8,128)S(1)}, f32[10,10,1]{2,1,0:T(8,128)S(1)}, u32[]{:S(2)}, u32[]{:S(2)}) collective-permute-start(f32[10,10,1]{2,1,0:T(8,128)S(1)} %get-tuple-element.182), channel_id=1, source_target_pairs={{1,0},{2,1},{3,2},{5,4},{6,5},{7,6},{9,8},{10,9},{11,10},{13,12},{... | collective-permute-start | bytes 1208 | tf_op jit(solution)/shard_map/ppermute | solution.py:22
  150.3 18.3 %collective-permute-start.29 = (f32[10,10,1]{2,1,0:T(8,128)S(1)}, f32[10,10,1]{2,1,0:T(8,128)S(1)}, u32[]{:S(2)}, u32[]{:S(2)}) collective-permute-start(f32[10,10,1]{2,1,0:T(8,128)S(1)} %get-tuple-element.181), channel_id=1, source_target_pairs={{0,1},{1,2},{2,3},{4,5},{5,6},{6,7},{8,9},{9,10},{10,11},{12,13},{... | collective-permute-start | bytes 1208 | tf_op jit(solution)/shard_map/ppermute | solution.py:19
  199.7 7.8 collective-permute-start.44
  223.4 7.8 collective-permute-start.50
  232.1 12.9 %collective-permute-start.52 = (f32[10,10,1]{2,1,0:T(8,128)S(1)}, f32[10,10,1]{2,1,0:T(8,128)S(1)}, u32[]{:S(2)}, u32[]{:S(2)}) collective-permute-start(f32[10,10,1]{2,1,0:T(8,128)S(1)} %get-tuple-element.175), channel_id=1, source_target_pairs={{1,0},{2,1},{3,2},{5,4},{6,5},{7,6},{9,8},{10,9},{11,10},{13,12},{... | collective-permute-start | bytes 1208 | tf_op jit(solution)/shard_map/ppermute | solution.py:22
  233.4 11.7 %collective-permute-start.53 = (f32[10,10,1]{2,1,0:T(8,128)S(1)}, f32[10,10,1]{2,1,0:T(8,128)S(1)}, u32[]{:S(2)}, u32[]{:S(2)}) collective-permute-start(f32[10,10,1]{2,1,0:T(8,128)S(1)} %get-tuple-element.176), channel_id=1, source_target_pairs={{0,1},{1,2},{2,3},{4,5},{5,6},{6,7},{8,9},{9,10},{10,11},{12,13},{... | collective-permute-start | bytes 1208 | tf_op jit(solution)/shard_map/ppermute | solution.py:19
  238.1 14.2 %collective-permute-start.54 = (f32[1,4,32]{2,1,0:T(4,128)S(1)}, f32[1,4,32]{2,1,0:T(4,128)S(1)}, u32[]{:S(2)}, u32[]{:S(2)}) collective-permute-start(f32[1,4,32]{2,1,0:T(4,128)S(1)} %get-tuple-element.292), channel_id=1, source_target_pairs={{32,0},{64,32},{96,64},{128,96},{160,128},{192,160},{224,192},{256... | collective-permute-start | bytes 1544 | tf_op jit(solution)/shard_map/ppermute | solution.py:22
  239.4 12.9 %collective-permute-start.55 = (f32[1,4,32]{2,1,0:T(4,128)S(1)}, f32[1,4,32]{2,1,0:T(4,128)S(1)}, u32[]{:S(2)}, u32[]{:S(2)}) collective-permute-start(f32[1,4,32]{2,1,0:T(4,128)S(1)} %get-tuple-element.293), channel_id=1, source_target_pairs={{0,32},{32,64},{64,96},{96,128},{128,160},{160,192},{192,224},{224... | collective-permute-start | bytes 1544 | tf_op jit(solution)/shard_map/ppermute | solution.py:19
  245.2 14.1 %collective-permute-start.60 = (f32[1,8,64]{2,1,0:T(8,128)S(1)}, f32[1,8,64]{2,1,0:T(8,128)S(1)}, u32[]{:S(2)}, u32[]{:S(2)}) collective-permute-start(f32[1,8,64]{2,1,0:T(8,128)S(1)} %get-tuple-element.213), channel_id=1, source_target_pairs={{32,0},{64,32},{96,64},{128,96},{160,128},{192,160},{224,192},{256... | collective-permute-start | bytes 6152 | tf_op jit(solution)/shard_map/ppermute | solution.py:22
  246.5 12.8 %collective-permute-start.61 = (f32[1,8,64]{2,1,0:T(8,128)S(1)}, f32[1,8,64]{2,1,0:T(8,128)S(1)}, u32[]{:S(2)}, u32[]{:S(2)}) collective-permute-start(f32[1,8,64]{2,1,0:T(8,128)S(1)} %get-tuple-element.212), channel_id=1, source_target_pairs={{0,32},{32,64},{64,96},{96,128},{128,160},{160,192},{192,224},{224... | collective-permute-start | bytes 6152 | tf_op jit(solution)/shard_map/ppermute | solution.py:19
  252.3 12.6 %collective-permute-start.56 = (f32[6,1,32]{2,1,0:T(1,128)S(1)}, f32[6,1,32]{2,1,0:T(1,128)S(1)}, u32[]{:S(2)}, u32[]{:S(2)}) collective-permute-start(f32[6,1,32]{2,1,0:T(1,128)S(1)} %get-tuple-element.257), channel_id=1, source_target_pairs={{4,0},{8,4},{12,8},{16,12},{20,16},{24,20},{28,24},{5,1},{9,5},{13... | collective-permute-start | bytes 2312 | tf_op jit(solution)/shard_map/ppermute | solution.py:22
  254.2 10.7 %collective-permute-start.57 = (f32[6,1,32]{2,1,0:T(1,128)S(1)}, f32[6,1,32]{2,1,0:T(1,128)S(1)}, u32[]{:S(2)}, u32[]{:S(2)}) collective-permute-start(f32[6,1,32]{2,1,0:T(1,128)S(1)} %get-tuple-element.256), channel_id=1, source_target_pairs={{0,4},{4,8},{8,12},{12,16},{16,20},{20,24},{24,28},{1,5},{5,9},{9,... | collective-permute-start | bytes 2312 | tf_op jit(solution)/shard_map/ppermute | solution.py:19
  265.8 11.4 %collective-permute-start.64 = (f32[10,10,1]{2,1,0:T(8,128)S(1)}, f32[10,10,1]{2,1,0:T(8,128)S(1)}, u32[]{:S(2)}, u32[]{:S(2)}) collective-permute-start(f32[10,10,1]{2,1,0:T(8,128)S(1)} %get-tuple-element.173), channel_id=1, source_target_pairs={{1,0},{2,1},{3,2},{5,4},{6,5},{7,6},{9,8},{10,9},{11,10},{13,12},{... | collective-permute-start | bytes 1208 | tf_op jit(solution)/shard_map/ppermute | solution.py:22
  267.1 10.1 %collective-permute-start.65 = (f32[10,10,1]{2,1,0:T(8,128)S(1)}, f32[10,10,1]{2,1,0:T(8,128)S(1)}, u32[]{:S(2)}, u32[]{:S(2)}) collective-permute-start(f32[10,10,1]{2,1,0:T(8,128)S(1)} %get-tuple-element.174), channel_id=1, source_target_pairs={{0,1},{1,2},{2,3},{4,5},{5,6},{6,7},{8,9},{9,10},{10,11},{12,13},{... | collective-permute-start | bytes 1208 | tf_op jit(solution)/shard_map/ppermute | solution.py:19
  286.5 14.7 %collective-permute-start.68 = (f32[6,1,32]{2,1,0:T(1,128)S(1)}, f32[6,1,32]{2,1,0:T(1,128)S(1)}, u32[]{:S(2)}, u32[]{:S(2)}) collective-permute-start(f32[6,1,32]{2,1,0:T(1,128)S(1)} %get-tuple-element.255), channel_id=1, source_target_pairs={{4,0},{8,4},{12,8},{16,12},{20,16},{24,20},{28,24},{5,1},{9,5},{13... | collective-permute-start | bytes 2312 | tf_op jit(solution)/shard_map/ppermute | solution.py:22
  288.7 12.4 %collective-permute-start.69 = (f32[6,1,32]{2,1,0:T(1,128)S(1)}, f32[6,1,32]{2,1,0:T(1,128)S(1)}, u32[]{:S(2)}, u32[]{:S(2)}) collective-permute-start(f32[6,1,32]{2,1,0:T(1,128)S(1)} %get-tuple-element.254), channel_id=1, source_target_pairs={{0,4},{4,8},{8,12},{12,16},{16,20},{20,24},{24,28},{1,5},{5,9},{9,... | collective-permute-start | bytes 2312 | tf_op jit(solution)/shard_map/ppermute | solution.py:19
  294.1 42.5 %collective-permute-start.84 = (f32[1,2,16]{2,1,0:T(2,128)S(1)}, f32[1,2,16]{2,1,0:T(2,128)S(1)}, u32[]{:S(2)}, u32[]{:S(2)}) collective-permute-start(f32[1,2,16]{2,1,0:T(2,128)S(1)} %get-tuple-element.330), channel_id=1, source_target_pairs={{32,0},{64,32},{96,64},{128,96},{160,128},{192,160},{224,192},{256... | collective-permute-start | bytes 392 | tf_op jit(solution)/shard_map/ppermute | solution.py:22
  295.4 41.2 %collective-permute-start.85 = (f32[1,2,16]{2,1,0:T(2,128)S(1)}, f32[1,2,16]{2,1,0:T(2,128)S(1)}, u32[]{:S(2)}, u32[]{:S(2)}) collective-permute-start(f32[1,2,16]{2,1,0:T(2,128)S(1)} %get-tuple-element.331), channel_id=1, source_target_pairs={{0,32},{32,64},{64,96},{96,128},{128,160},{160,192},{192,224},{224... | collective-permute-start | bytes 392 | tf_op jit(solution)/shard_map/ppermute | solution.py:19
  337.3 9.8 collective-permute-start.80
  339.2 7.9 collective-permute-start.81
  345.1 19.0 %collective-permute-start.86 = (f32[4,1,16]{2,1,0:T(1,128)S(1)}, f32[4,1,16]{2,1,0:T(1,128)S(1)}, u32[]{:S(2)}, u32[]{:S(2)}) collective-permute-start(f32[4,1,16]{2,1,0:T(1,128)S(1)} %get-tuple-element.311), channel_id=1, source_target_pairs={{4,0},{8,4},{12,8},{16,12},{20,16},{24,20},{28,24},{5,1},{9,5},{13... | collective-permute-start | bytes 776 | tf_op jit(solution)/shard_map/ppermute | solution.py:22
  347.2 9.8 collective-permute-start.82
  348.5 8.5 collective-permute-start.83
  353.1 11.1 %collective-permute-start.87 = (f32[4,1,16]{2,1,0:T(1,128)S(1)}, f32[4,1,16]{2,1,0:T(1,128)S(1)}, u32[]{:S(2)}, u32[]{:S(2)}) collective-permute-start(f32[4,1,16]{2,1,0:T(1,128)S(1)} %get-tuple-element.310), channel_id=1, source_target_pairs={{0,4},{4,8},{8,12},{12,16},{16,20},{20,24},{24,28},{1,5},{5,9},{9,... | collective-permute-start | bytes 776 | tf_op jit(solution)/shard_map/ppermute | solution.py:19
  370.6 11.6 %collective-permute-start.88 = (f32[4,4,1]{2,1,0:T(4,128)S(1)}, f32[4,4,1]{2,1,0:T(4,128)S(1)}, u32[]{:S(2)}, u32[]{:S(2)}) collective-permute-start(f32[4,4,1]{2,1,0:T(4,128)S(1)} %get-tuple-element.283), channel_id=1, source_target_pairs={{1,0},{2,1},{3,2},{5,4},{6,5},{7,6},{9,8},{10,9},{11,10},{13,12},{... | collective-permute-start | bytes 200 | tf_op jit(solution)/shard_map/ppermute | solution.py:22
  372.0 9.8 collective-permute-start.94
  373.3 8.6 collective-permute-start.95
  412.3 7.8 collective-permute-start.104
  435.4 7.8 collective-permute-start.110
  647.4 8.1 collective-permute-start.128
  669.6 7.8 collective-permute-start.134
  691.5 7.8 collective-permute-start.140
  713.6 7.8 collective-permute-start.146
  735.8 7.8 collective-permute-start.152
  759.1 7.8 collective-permute-start.158
  782.5 8.1 collective-permute-start.164
  806.7 7.8 collective-permute-start.170
  830.6 7.8 collective-permute-start.176
  854.7 7.8 collective-permute-start.182
  878.7 7.8 collective-permute-start.188
  913.6 7.8 collective-permute-start.194
  939.3 7.8 collective-permute-start.200
  965.1 9.0 collective-permute-start.206
  967.0 7.9 collective-permute-start.207
  992.1 7.8 collective-permute-start.212
  (154 other events, 1054.3 us)
where the time goes:
time: 1030 us; the launch traced here: 1010 us
  starting transfers between devices  711 us (69%)
  blocking collectives  116 us (11%)
  waiting for transfers between devices  89.7 us (9%)
  local copies, waits for them, and re-layouts  39.2 us (4%)
  other arithmetic  31 us (3%)
  between operations  23.5 us (2%)
    ppermute x108, starting transfers between devices, padded_2(): lax.ppermute(lax.slice_in_dim(block, block.shape[dim] - width, None, axis...  534 us
    ppermute x108, starting transfers between devices, padded_2(): lax.ppermute(lax.slice_in_dim(block, 0, width, axis=dim), axis, backward)  177 us
    unnamed x1, blocking collectives  116 us
    ppermute x108, waiting for transfers between devices, padded_2(): lax.ppermute(lax.slice_in_dim(block, block.shape[dim] - width, None, axis...  70.6 us
    reshape x4, local copies, waits for them, and re-layouts, coarsen(): field.reshape(size_a // 2, 2, size_b // 2, 2, size_c // 2, 2)  20.7 us
  transfers between devices with their start and end apart: 216, of which 95 were waited for; matrix products, arithmetic and copies ran while one was open for 3% of the time, Pallas kernels for 0%

commit v1 on v0

v1 whole, which is shorter than its diff:
```python
import functools

import jax
import jax.numpy as jnp
from jax import lax
from jax.experimental import pallas as pl
from jax.experimental.pallas import tpu as pltpu
from jax.sharding import PartitionSpec as P

F32 = jnp.float32
MESH = pl.DeviceIdType.MESH
CG_ITERS = 8
THETA = 1.125
DELTA = 0.875

H0, H0R = 5, 3
H1K, H1F, H1R = 6, 4, 5


def cheb_table():
    sigma = THETA / DELTA
    rho_now = 1.0 / sigma
    table = []
    for _ in range(3):
        rho_next = 1.0 / (2.0 * sigma - rho_now)
        table.append((rho_next * rho_now, 2.0 * rho_next / DELTA))
        rho_now = rho_next
    return table


TABLE = cheb_table()


def mm(a, b):
    return jnp.dot(a, b, precision=lax.Precision.HIGHEST, preferred_element_type=F32)


def iota(shape, dim):
    return lax.broadcasted_iota(jnp.int32, shape, dim)


def flat(v):
    return v.reshape(v.shape[0] * v.shape[1], v.shape[2])


def up(v, dim, step=1):
    return pltpu.roll(v, v.shape[dim] - step, dim)


def down(v, dim, step=1):
    return pltpu.roll(v, step, dim)


def planes_loop(lo, hi, group, fn):
    count = (hi - lo) // group
    if count > 1:
        def body(i, carry):
            fn(lo + i * group, group)
            return carry

        lax.fori_loop(0, count, body, 0)
    elif count == 1:
        fn(lo, group)
    rest = hi - lo - count * group
    if rest:
        fn(lo + count * group, rest)


def weights(lev, lo, hi, h, whole, group):
    K = lev["K"]
    rows, lanes = K.shape[1], K.shape[2]

    def one(p, g):
        n = g * rows
        k = flat(K[pl.ds(p, g)])
        kxu = flat(K[pl.ds(p + 1, g)])
        kxd = flat(K[pl.ds(p - 1, g)])
        kyu, kyd, kzu, kzd = up(k, 0), down(k, 0), up(k, 1), down(k, 1)
        if whole:
            row = iota((n, lanes), 0) & (rows - 1)
            lane = iota((n, lanes), 1)
            kyu = jnp.where(row == rows - 1, 0.0, kyu)
            kyd = jnp.where(row == 0, 0.0, kyd)
            kzu = jnp.where(lane == lanes - 1, 0.0, kzu)
            kzd = jnp.where(lane == 0, 0.0, kzd)
        wy, wz = h * (k + kyu), h * (k + kzu)
        diag = h * (6.0 * k + ((kxu + kxd) + (kyu + kyd) + (kzu + kzd)))
        if whole:
            wy = jnp.where(row == rows - 1, 0.0, wy)
            wz = jnp.where(lane == lanes - 1, 0.0, wz)
        shape = (g, rows, lanes)
        lev["WX"][pl.ds(p, g)] = (h * (k + kxu)).reshape(shape)
        lev["WY"][pl.ds(p, g)] = wy.reshape(shape)
        lev["WZ"][pl.ds(p, g)] = wz.reshape(shape)
        lev["DG"][pl.ds(p, g)] = diag.reshape(shape)
        lev["IV"][pl.ds(p, g)] = jnp.where(k > 0.0, 1.0 / diag, 0.0).reshape(shape)

    lev["WX"][lo - 1] = h * (K[lo - 1] + K[lo])
    planes_loop(lo, hi, group, one)


def sweep(lev, R, X, src, dst, lo, hi, a, b, group, first=False, want_dir=True):
    Vi, Vo = lev[src], lev[dst]
    rows, lanes = Vi.shape[1], Vi.shape[2]

    def one(p, g):
        here = pl.ds(p, g)
        shape = (g, rows, lanes)
        v = flat(Vi[here])
        total = flat(lev["WX"][here]) * flat(Vi[pl.ds(p + 1, g)])
        total = total + flat(lev["WX"][pl.ds(p - 1, g)]) * flat(Vi[pl.ds(p - 1, g)])
        wy, wz = flat(lev["WY"][here]), flat(lev["WZ"][here])
        total = total + (wy * up(v, 0) + down(wy * v, 0))
        total = total + (wz * up(v, 1) + down(wz * v, 1))
        r = flat(R[here]) - (flat(lev["DG"][here]) * v - total)
        R[here] = r.reshape(shape)
        if first:
            X[here] = v.reshape(shape)
        else:
            X[here] = X[here] + v.reshape(shape)
        if want_dir:
            d = b * (flat(lev["IV"][here]) * r)
            if a:
                d = d + a * v
            Vo[here] = d.reshape(shape)

    planes_loop(lo, hi, group, one)


def presmooth(lev, R, X, halos, base, own, group, whole=False):
    h = 0 if whole else halos[0] + 1
    lo, hi = base - h, base + own + h

    def start(p, g):
        here = pl.ds(p, g)
        lev["Va"][here] = (lev["IV"][here] * R[here]) * (1.0 / THETA)

    planes_loop(lo, hi, group, start)
    names = ("Va", "Vb")
    for j in range(4):
        a, b = TABLE[j] if j < 3 else (0.0, 0.0)
        lo, hi = base - halos[j], base + own + halos[j]
        sweep(lev, R, X, names[j % 2], names[1 - j % 2], lo, hi, a, b, group,
              first=(j == 0), want_dir=(j < 3))


def postsmooth(lev, R, X, halos, base, own, group):
    names = ("Va", "Vb")
    for j in range(4):
        a, b = TABLE[j - 1] if j > 0 else (0.0, 1.0 / THETA)
        lo, hi = base - halos[j], base + own + halos[j]
        sweep(lev, R, X, names[j % 2], names[1 - j % 2], lo, hi, a, b, group)


def kernel(sizes, names, *refs):
    f_ref, k_ref, out_ref = refs[:3]
    S = dict(zip(names, refs[3:]))
    ss, rs = S["ss"], S["rs"]
    NGX, NGY, NGZ = sizes
    NYC = NGY // 2
    NX0, NY0, NZ0 = 16 * NGX, 16 * NGY, 128 * NGZ
    NX1, NY1, NZ1 = NX0 // 2, NY0 // 2, NZ0 // 2
    NX3 = 2 * NGX
    gx, gy, gz = lax.axis_index("gx"), lax.axis_index("gy"), lax.axis_index("gz")
    core, chip = gy % 2, gy // 2

    def at(dx=0, dy=0, dz=0):
        return ((gx + dx + NGX) % NGX, (gy + dy + NGY) % NGY, (gz + dz + NGZ) % NGZ)

    pair_peers = [(c, dz) for c in (0, 1) for dz in range(NGZ) if (c, dz) != (0, 0)]

    def pair_dev(c, dz):
        return (gx, chip * 2 + (core + c) % 2, (gz + dz) % NGZ)

    def chip_dev(dy):
        return (gx, ((chip + dy) % NYC) * 2 + core, gz)

    sides = [(dx, dy) for dx in (-1, 0, 1) for dy in (-1, 0, 1) if (dx, dy) != (0, 0)]

    barrier = pltpu.get_barrier_semaphore()
    greeted = [pair_dev(c, dz) for c, dz in pair_peers]
    greeted += [chip_dev(dy) for dy in range(1, NYC)]
    greeted += [at(dx=d) for d in range(1, NGX)]
    greeted += [at(dx=dx, dy=dy) for dx, dy in sides if dy != 0]
    for dev in greeted:
        pl.semaphore_signal(barrier, inc=1, device_id=dev, device_id_type=MESH)

    counter = [0]

    def remote(src, dst, dev):
        i = counter[0]
        counter[0] += 1
        return pltpu.make_async_remote_copy(
            src_ref=src, dst_ref=dst, send_sem=ss.at[i], recv_sem=rs.at[i],
            device_id=dev, device_id_type=MESH,
        )

    def begin(copies):
        for c in copies:
            c.start()
        return copies

    def finish(copies):
        for c in copies:
            c.wait()

    def z_copies(buf, from_left, from_right):
        return [remote(buf, from_left, at(dz=1)), remote(buf, from_right, at(dz=-1))]

    def xy_copies(buf, base, own, h, rows):
        fields = slice(None)
        xs = {1: (base + own - h, base - h, h), -1: (base, base + own, h), 0: (base, base, own)}
        ys = {1: (rows, 0, 8), -1: (8, 8 + rows, 8), 0: (8, 8, rows)}
        out = []
        for dx, dy in sides:
            (sx, tx, nx), (sy, ty, ny) = xs[dx], ys[dy]
            out.append(remote(
                buf.at[fields, pl.ds(sx, nx), pl.ds(sy, ny)],
                buf.at[fields, pl.ds(tx, nx), pl.ds(ty, ny)],
                at(dx=dx, dy=dy)))
        return out

    def x_copies(buf, n1, n2):
        out = []
        for d, n in ((1, n1), (2, n2)):
            if n:
                out.append(remote(buf.at[:, pl.ds(11 - n, n)],
                                  buf.at[:, pl.ds(7 - 4 * (d - 1) - n, n)], at(dx=d)))
                out.append(remote(buf.at[:, pl.ds(7, n)],
                                  buf.at[:, pl.ds(11 + 4 * (d - 1), n)], at(dx=-d)))
        return out

    def pair_copies(buf, slots):
        return [remote(buf, slots.at[i], pair_dev(c, dz)) for i, (c, dz) in enumerate(pair_peers)]

    def chip_copies(buf):
        mine = buf.at[0, pl.ds(7, 4), pl.ds(pl.multiple_of(chip * 8, 8), 8)]
        return [remote(mine, mine, chip_dev(dy)) for dy in range(1, NYC)]

    def gather_copies(buf):
        return [remote(buf.at[gx], buf.at[gx], at(dx=d)) for d in range(1, NGX)]

    lane16 = iota((16, 128), 1)
    lane8 = iota((8, 128), 1)

    def sel(shape, cond, value):
        return jnp.where(cond(iota(shape, 0), iota(shape, 1)), value, 0.0).astype(F32)

    def coarse_0(r):
        c = sel((64, 256), lambda r, c: ((c >> 5) == (r >> 3)) & (((c & 15) >> 1) == (r & 7)), 0.25)
        z = sel((128, 128), lambda l, c: (l >> 1) == (c & 63), 0.5)
        return mm(mm(c, r), z)

    def coarse_1(r):
        c = sel((32, 64), lambda r, c: ((c >> 4) == (r >> 3)) & (((c & 7) >> 1) == (r & 7) - 4 * core), 0.25)
        z = sel((128, 128), lambda l, c: (l < 64) & (c == 32 * gz + (l >> 1)), 0.5)
        return mm(mm(c, r), z)

    def coarse_2(r):
        c = sel((32, 128), lambda r, c: ((c >> 6) == (r >> 4)) & (((c & 31) >> 1) == (r & 15)), 0.25)
        z = sel((128, 128), lambda l, c: (l >> 1) == (c & 63), 0.5)
        t = mm(mm(c, r), z)
        return jnp.where(lane16 < 64, t[0:16], t[16:32])

    def coarse_3(r):
        n = r.shape[0]
        c = sel((n // 4, n), lambda r, c: ((c >> 5) == (r >> 3)) & (((c & 15) >> 1) == (r & 7)), 0.25)
        z = sel((128, 128), lambda l, c: (l < 64) & ((l >> 1) == c), 0.5)
        return mm(mm(c, r), z)

    def fine_3(e):
        n = e.shape[0]
        u = sel((4 * n, n), lambda r, c: ((r >> 5) == (c >> 3)) & (((r & 15) >> 1) == (c & 7)), 1.0)
        z = sel((128, 128), lambda c, l: (l < 64) & ((l >> 1) == c), 1.0)
        return mm(u, mm(e, z))

    def pack0(field):
        out = []
        for g in range(2):
            acc = None
            for j in range(8):
                t = pltpu.roll(field(8 * g + j), 16 * j + 8, 1)
                acc = t if acc is None else jnp.where((lane16 >> 4) == j, t, acc)
            out.append(acc)
        return out

    def centre0(buf, fld, h, field, from_left, from_right):
        base = h + 1
        for g, m in ((0, base), (1, base + 17)):
            buf[fld, m, 8:24] = jnp.where((lane16 & 15) >= 8, from_right[fld, g], from_left[fld, g])

    def body0(buf, fld, h, ref):
        base = h + 1
        buf[fld, base + 1:base + 17, 8:24] = ref[...]

    def unpack0(buf, fld, h, lo, hi, put):
        for x in range(lo, hi):
            if x < 0:
                main, m, j = x + h, h, x + 8
            elif x < 16:
                main, m, j = h + 2 + x, (h + 1 if x < 8 else h + 18), x % 8
            else:
                main, m, j = h + 20 + x - 16, h + 19, x - 16
            put(x, buf[fld, main], pltpu.roll(buf[fld, m], (120 - 16 * j) % 128, 1))

    def double1(v):
        n = v.shape[0]
        return jnp.where(iota((n, 128), 1) < 64, v, pltpu.roll(v, 64, 1))

    def centre1(buf, fld, own, left, right, i):
        lane = iota((64, 128), 1)
        t = jnp.where(lane < 64, flat(own[i]), jnp.where(lane < 96, flat(right[i]), flat(left[i])))
        buf[fld, 6:14, 8:16] = t.reshape(8, 8, 128)

    def inside(n_rows, n_lanes, row0, lane_of, ny, nz):
        y = iota((n_rows, n_lanes), 0) + row0
        z = lane_of(iota((n_rows, n_lanes), 1))
        return jnp.where((y >= 0) & (y < ny) & (z >= 0) & (z < nz), 1.0, 0.0).astype(F32)

    def xin(x, n):
        return jnp.where((x >= 0) & (x < n), 1.0, 0.0).astype(F32)

    L0 = {n: S[n + "0"] for n in ("K", "WX", "WY", "WZ", "DG", "IV", "Va", "Vb")}
    L1 = {n: S[n + "1"] for n in ("WX", "WY", "WZ", "DG", "IV", "Va", "Vb")}
    L1["K"] = S["K1"].at[0]
    L2 = {n: S[n + "2"] for n in ("WX", "WY", "WZ", "DG", "IV", "Va", "Vb")}
    L2["K"] = S["K2"].at[0]
    L3 = {n: S[n + "3"] for n in ("K", "WX", "WY", "WZ", "DG", "IV", "Va", "Vb")}
    R0, X0 = S["R0"], S["X0"]
    F1, X1 = S["F1"].at[0], S["X1"]
    F2, X2 = S["F2"].at[0], S["X2"]
    F3, X3 = S["F3"], S["X3"]

    E0, E0r = S["E0"], S["E0r"]
    for fld, ref in ((0, f_ref), (1, k_ref)):
        for g, t in enumerate(pack0(lambda x: ref[x])):
            S["P0"][fld, g] = t
        body0(E0, fld, H0, ref)
    k1 = coarse_0(k_ref[...].reshape(256, 128))
    S["T1k"][0] = k1.reshape(8, 8, 128)
    S["B2k"][...] = coarse_1(k1).reshape(4, 8, 128)

    pl.semaphore_wait(barrier, len(greeted))
    z0 = begin(z_copies(S["P0"], S["P0L"], S["P0R"]))
    z1k = begin(z_copies(S["T1k"], S["T1kL"], S["T1kR"]))
    p2k = begin(pair_copies(S["B2k"], S["B2kS"]))

    finish(z0)
    for fld in (0, 1):
        centre0(E0, fld, H0, None, S["P0L"], S["P0R"])
    xy0 = begin(xy_copies(E0, H0 + 1, 18, H0 + 1, 16))
    finish(z1k)
    centre1(S["K1"], 0, S["T1k"], S["T1kL"], S["T1kR"], 0)
    xy1k = begin(xy_copies(S["K1"], 6, 8, H1K, 8))
    finish(p2k)

    def pair_sum(own, slots):
        total = own[...]
        for i in range(len(pair_peers)):
            total = total + slots[i]
        return total

    my_rows = pl.ds(pl.multiple_of(chip * 8, 8), 8)
    if NYC * 8 < 32:
        S["K2"][...] = jnp.zeros(S["K2"].shape, F32)
        S["F2"][...] = jnp.zeros(S["F2"].shape, F32)
    S["K2"][0, 7:11, my_rows] = pair_sum(S["B2k"], S["B2kS"])
    c2k = begin(chip_copies(S["K2"]))

    finish(xy0)

    def lane0(l):
        return 128 * gz + jnp.where(l < 192, l, l - 256)

    in0 = inside(32, 256, 16 * gy - 8, lane0, NY0, NZ0)

    def put_k(x, main, halo):
        w = xin(16 * gx + x, NX0)
        L0["K"][x + 5, :, 0:128] = main * (in0[:, 0:128] * w)
        L0["K"][x + 5, :, 128:256] = halo * (in0[:, 128:256] * w)

    def put_r(x, main, halo):
        R0[x + 5, :, 0:128] = main
        R0[x + 5, :, 128:256] = halo

    unpack0(E0, 1, H0, -5, 21, put_k)
    unpack0(E0, 0, H0, -4, 20, put_r)
    weights(L0, 1, 25, 0.5, False, 1)

    finish(c2k)
    xx2k = begin(x_copies(S["K2"], 4, 3))
    S["G3k"][gx] = coarse_2(S["K2"][0, 7:11].reshape(128, 128))
    g3k = begin(gather_copies(S["G3k"]))

    presmooth(L0, R0, X0, (3, 2, 1, 0), 5, 16, 1)

    own0 = R0[5:21, 8:24, 0:128]
    S["T1f"][0] = coarse_0(own0.reshape(256, 128)).reshape(8, 8, 128)
    z1f = begin(z_copies(S["T1f"], S["T1fL"], S["T1fR"]))
    for g, t in enumerate(pack0(lambda x: R0[5 + x, 8:24, 0:128])):
        S["P0r"][0, g] = t
    E0r[0, H0R + 2:H0R + 18, 8:24] = own0
    z0r = begin(z_copies(S["P0r"], S["P0rL"], S["P0rR"]))

    finish(xy1k)

    def lane1(l):
        return 64 * gz + jnp.where(l < 96, l, l - 128)

    in1 = inside(24, 128, 8 * gy - 8, lane1, NY1, NZ1)
    for p in range(20):
        L1["K"][p] = L1["K"][p] * (in1 * xin(8 * gx + p - 6, NX1))
    weights(L1, 1, 19, 0.5 * 0.25, False, 2)

    finish(z1f)
    centre1(S["F1"], 0, S["T1f"], S["T1fL"], S["T1fR"], 0)
    xy1f = begin(xy_copies(S["F1"], 6, 8, H1F, 8))
    finish(z0r)
    centre0(E0r, 0, H0R, None, S["P0rL"], S["P0rR"])
    xy0r = begin(xy_copies(E0r, H0R + 1, 18, H0R + 1, 16))
    finish(xy1f)
    presmooth(L1, F1, X1, (3, 2, 1, 0), 6, 8, 2)

    r1 = F1[6:14, 8:16]
    S["B2f"][...] = coarse_1(r1.reshape(64, 128)).reshape(4, 8, 128)
    p2f = begin(pair_copies(S["B2f"], S["B2fS"]))
    S["T1r"][0] = double1(r1.reshape(64, 128)).reshape(8, 8, 128)
    S["T1r"][1] = double1(X1[6:14, 8:16].reshape(64, 128)).reshape(8, 8, 128)
    z1r = begin(z_copies(S["T1r"], S["T1rL"], S["T1rR"]))

    finish(xx2k)
    for p in range(18):
        if p < 7 or p > 10:
            L2["K"][p] = L2["K"][p] * xin(4 * gx + p - 7, NX1 // 2)
    weights(L2, 1, 17, 0.5 * 0.25 ** 2, True, 2)

    finish(p2f)
    S["F2"][0, 7:11, my_rows] = pair_sum(S["B2f"], S["B2fS"])
    c2f = begin(chip_copies(S["F2"]))
    finish(z1r)
    for i in (0, 1):
        centre1(S["RX1"], i, S["T1r"], S["T1rL"], S["T1rR"], i)
    finish(c2f)
    xx2f = begin(x_copies(S["F2"], 4, 0))
    xy1r = begin(xy_copies(S["RX1"], 6, 8, H1R, 8))

    finish(g3k)

    def unpack3(slots, dst):
        for s in range(NGX):
            t = slots[s]
            dst[5 + 2 * s] = jnp.where(lane16 < 64, t, 0.0)
            dst[6 + 2 * s] = jnp.where(lane16 < 64, pltpu.roll(t, 64, 1), 0.0)

    unpack3(S["G3k"], L3["K"])
    zero3 = jnp.zeros((5, 16, 128), F32)
    for ref in (L3["K"], L3["Va"], L3["Vb"], X3):
        ref[0:5] = zero3
        ref[5 + NX3:10 + NX3] = zero3
    weights(L3, 5, 5 + NX3, 0.5 * 0.25 ** 3, True, 4)

    finish(xx2f)
    presmooth(L2, F2, X2, (3, 2, 1, 0), 7, 4, 2)

    S["G3f"][gx] = coarse_2(F2[7:11].reshape(128, 128))
    g3f = begin(gather_copies(S["G3f"]))
    S["RX2"][0, 7:11] = F2[7:11]
    S["RX2"][1, 7:11] = X2[7:11]
    xx2r = begin(x_copies(S["RX2"], 4, 2))

    n4 = 8 * (NX3 // 2)
    h4 = 0.5 * 0.25 ** 4
    k4 = coarse_3(L3["K"][5:5 + NX3].reshape(16 * NX3, 128))
    row4 = iota((n4, 128), 0)
    plane_end = (row4 & 7) == 7
    last_plane = row4 >= n4 - 8
    first_plane = row4 < 8
    k4xu = jnp.where(last_plane, 0.0, up(k4, 0, 8))
    k4xd = jnp.where(first_plane, 0.0, down(k4, 0, 8))
    k4yu = jnp.where(plane_end, 0.0, up(k4, 0))
    k4yd = jnp.where((row4 & 7) == 0, 0.0, down(k4, 0))
    k4zu, k4zd = up(k4, 1), down(k4, 1)
    wx4 = jnp.where(last_plane, 0.0, h4 * (k4 + k4xu))
    wy4 = jnp.where(plane_end, 0.0, h4 * (k4 + k4yu))
    wz4 = h4 * (k4 + k4zu)
    dg4 = h4 * (6.0 * k4 + ((k4xu + k4xd) + (k4yu + k4yd) + (k4zu + k4zd)))

    finish(g3f)
    unpack3(S["G3f"], F3)
    presmooth(L3, F3, X3, (0, 0, 0, 0), 5, NX3, 4, whole=True)

    f4 = coarse_3(F3[5:5 + NX3].reshape(16 * NX3, 128))
    f4 = jnp.where(k4 > 0.0, f4, 0.0)
    x4 = jnp.zeros_like(f4)
    r4 = p4 = f4
    rr = jnp.sum(r4 * r4, keepdims=True)
    for _ in range(CG_ITERS):
        q4 = dg4 * p4 - (
            (wx4 * up(p4, 0, 8) + down(wx4 * p4, 0, 8))
            + (wy4 * up(p4, 0) + down(wy4 * p4, 0))
            + (wz4 * up(p4, 1) + down(wz4 * p4, 1)))
        q4 = jnp.where(k4 > 0.0, q4, 0.0)
        alpha = rr / jnp.sum(p4 * q4, keepdims=True)
        x4 = x4 + alpha * p4
        r4 = r4 - alpha * q4
        rn = jnp.sum(r4 * r4, keepdims=True)
        p4 = r4 + (rn / rr) * p4
        rr = rn

    L3["Va"][5:5 + NX3] = fine_3(x4).reshape(NX3, 16, 128)
    postsmooth(L3, F3, X3, (0, 0, 0, 0), 5, NX3, 4)
    X3[5:5 + NX3] = X3[5:5 + NX3] + L3["Va"][5:5 + NX3]

    finish(xx2r)
    z3 = sel((128, 128), lambda c, l: (l >> 1) == c, 1.0)
    y3 = sel((32, 16), lambda r, c: (r >> 1) == c, 1.0)
    t = mm(X3[pl.ds(2 * gx + 1, 10)].reshape(160, 128), z3)
    for q in range(10):
        e = mm(y3, t[16 * q:16 * q + 16])
        for p in (2 * q - 1, 2 * q):
            if 0 <= p < 18:
                L2["Va"][p] = e
    R2b, X2b = S["RX2"].at[0], S["RX2"].at[1]
    postsmooth(L2, R2b, X2b, (6, 5, 4, 3), 7, 4, 2)
    X2b[4:14] = X2b[4:14] + L2["Va"][4:14]

    finish(xy1r)
    z2 = sel((128, 128), lambda c, l: ((lane1(l) >> 1) == c) & (lane1(l) >= 0) & (lane1(l) < NZ1), 1.0)

    def yrow(r):
        return 8 * gy + r - 8

    y2 = sel((24, 32), lambda r, c: ((yrow(r) >> 1) == c) & (yrow(r) >= 0) & (yrow(r) < NY1), 1.0)
    t = mm(X2b[4:14].reshape(320, 128), z2)
    for q in range(10):
        e = mm(y2, t[32 * q:32 * q + 32])
        e = e * xin(4 * gx + q - 3, NX1 // 2)
        L1["Va"][2 * q] = e
        L1["Va"][2 * q + 1] = e
    R1b, X1b = S["RX1"].at[0], S["RX1"].at[1]
    postsmooth(L1, R1b, X1b, (5, 4, 3, 2), 6, 8, 2)
    X1b[4:16] = X1b[4:16] + L1["Va"][4:16]

    finish(xy0r)
    unpack0(E0r, 0, H0R, -3, 19, put_r)

    def zfine(c, l):
        z = jnp.where(l < 192, l, l - 256)
        g = 128 * gz + z
        return (((z >> 1) & 127) == c) & (g >= 0) & (g < NZ0)

    def yfine(r, c):
        g = 16 * gy + r - 8
        return (((r - 8) >> 1) + 8 == c) & (g >= 0) & (g < NY0)

    z1 = sel((128, 256), zfine, 1.0)
    y1 = sel((32, 24), yfine, 1.0)
    t = mm(X1b[4:16].reshape(288, 128), z1)
    for q in range(12):
        e = mm(y1, t[24 * q:24 * q + 24])
        e = e * xin(8 * gx + q - 2, NX1)
        L0["Va"][1 + 2 * q] = e
        L0["Va"][2 + 2 * q] = e
    postsmooth(L0, R0, X0, (3, 2, 1, 0), 5, 16, 1)
    out_ref[...] = X0[5:21, 8:24, 0:128] + L0["Va"][5:21, 8:24, 0:128]


def scratch(sizes):
    ngx, ngy, ngz = sizes
    n_pair = 2 * ngz - 1
    shapes = {
        "P0": (2, 2, 16, 128), "P0L": (2, 2, 16, 128), "P0R": (2, 2, 16, 128),
        "E0": (2, 18 + 2 * (H0 + 1), 32, 128),
        "P0r": (1, 2, 16, 128), "P0rL": (1, 2, 16, 128), "P0rR": (1, 2, 16, 128),
        "E0r": (1, 18 + 2 * (H0R + 1), 32, 128),
        "R0": (26, 32, 256), "X0": (26, 32, 256), "K0": (26, 32, 256),
        "T1r": (2, 8, 8, 128), "T1rL": (2, 8, 8, 128), "T1rR": (2, 8, 8, 128),
        "K1": (1, 20, 24, 128), "F1": (1, 20, 24, 128), "RX1": (2, 20, 24, 128), "X1": (20, 24, 128),
        "K2": (1, 18, 32, 128), "F2": (1, 18, 32, 128), "RX2": (2, 18, 32, 128), "X2": (18, 32, 128),
        "B2k": (4, 8, 128), "B2kS": (n_pair, 4, 8, 128),
        "B2f": (4, 8, 128), "B2fS": (n_pair, 4, 8, 128),
        "G3k": (ngx, 16, 128), "G3f": (ngx, 16, 128),
        "K3": (2 * ngx + 10, 16, 128), "F3": (2 * ngx + 10, 16, 128), "X3": (2 * ngx + 10, 16, 128),
    }
    for n in ("T1k", "T1f"):
        for side in ("", "L", "R"):
            shapes[n + side] = (1, 8, 8, 128)
    for n in ("WX", "WY", "WZ", "DG", "IV", "Va", "Vb"):
        shapes[n + "0"] = (26, 32, 256)
        shapes[n + "1"] = (20, 24, 128)
        shapes[n + "2"] = (18, 32, 128)
        shapes[n + "3"] = (2 * ngx + 10, 16, 128)
    names = list(shapes) + ["ss", "rs"]
    n_sem = 4 * 10 + 10 + 2 * (n_pair + max(ngy // 2 - 1, 0)) + 4 + 2 + 4 + 2 * (ngx - 1)
    kinds = [pltpu.VMEM(shapes[n], F32) for n in shapes]
    kinds += [pltpu.SemaphoreType.DMA((n_sem,)), pltpu.SemaphoreType.DMA((n_sem,))]
    return names, kinds


def solution(mesh):
    sizes = (mesh.shape["gx"], mesh.shape["gy"], mesh.shape["gz"])
    names, kinds = scratch(sizes)
    spec = P("gx", "gy", "gz")

    def local(right_side, conductivity):
        return pl.pallas_call(
            functools.partial(kernel, sizes, names),
            out_shape=jax.ShapeDtypeStruct(right_side.shape, F32),
            in_specs=[pl.BlockSpec(memory_space=pltpu.VMEM)] * 2,
            out_specs=pl.BlockSpec(memory_space=pltpu.VMEM),
            scratch_shapes=kinds,
            compiler_params=pltpu.CompilerParams(
                collective_id=0, has_side_effects=True, vmem_limit_bytes=48 * 1024 * 1024
            ),
        )(right_side, conductivity)

    return jax.shard_map(local, mesh=mesh, in_specs=(spec, spec), out_specs=spec, check_vma=False)
```

time: 1030 us -> 100 us (0.10)
  the two profiles are of different devices: /device:TPU:1 before, /device:TPU:2 now
where the time goes in v1:
time: 100 us
  Pallas kernels  97.6 us (98%)
  local copies, waits for them, and re-layouts  2.47 us (2%)
    pallas_call x1, Pallas kernels, local(): pl.pallas_call(functools.partial(kernel, sizes, names), out_shape=jax.Sha...  97.6 us
    unnamed x5, local copies, waits for them, and re-layouts  2.47 us

profile of v1, /device:TPU:2, one launch (start us, length us, event | category | flops | bytes accessed | tf_op | source)
XLA Modules:
  0.0 100.1 jit_solution(9634482311118034867)
XLA Ops:
  0.0 0.0 copy-start
  0.0 0.9 copy-done
  0.9 0.0 copy-start.1
  0.9 0.9 copy-done.1
  1.8 97.6 %shard_map.28 = f32[16,16,128]{2,1,0:T(8,128)S(1)} custom-call(f32[16,16,128]{2,1,0:T(8,128)S(1)} %copy-done, f32[16,16,128]{2,1,0:T(8,128)S(1)} %copy-done.1), custom_call_target="tpu_custom_call" | custom-call | tf_op jit(solution)/shard_map/pallas_call | solution.py:606
  99.4 0.7 copy.4
Async XLA Ops:
  0.0 0.9 copy-start
  0.9 0.9 copy-start.1

commit v2 on v1

--- a/solution.py
+++ b/solution.py
@@ -15,6 +15,9 @@
 
 H0, H0R = 5, 3
 H1K, H1F, H1R = 6, 4, 5
+
+G0, G1, G2, G3 = 4, 8, 8, 16
+OWN0 = (slice(8, 24), slice(0, 128))
 
 
 def cheb_table():
@@ -99,35 +102,30 @@
     planes_loop(lo, hi, group, one)
 
 
-def sweep(lev, R, X, src, dst, lo, hi, a, b, group, first=False, want_dir=True):
+def sweep(lev, R, X, src, dst, lo, hi, a, b, group, first=False, want_dir=True, part=None):
     Vi, Vo = lev[src], lev[dst]
-    rows, lanes = Vi.shape[1], Vi.shape[2]
 
     def one(p, g):
-        here = pl.ds(p, g)
-        shape = (g, rows, lanes)
-        v = flat(Vi[here])
-        total = flat(lev["WX"][here]) * flat(Vi[pl.ds(p + 1, g)])
-        total = total + flat(lev["WX"][pl.ds(p - 1, g)]) * flat(Vi[pl.ds(p - 1, g)])
-        wy, wz = flat(lev["WY"][here]), flat(lev["WZ"][here])
-        total = total + (wy * up(v, 0) + down(wy * v, 0))
-        total = total + (wz * up(v, 1) + down(wz * v, 1))
-        r = flat(R[here]) - (flat(lev["DG"][here]) * v - total)
-        R[here] = r.reshape(shape)
-        if first:
-            X[here] = v.reshape(shape)
-        else:
-            X[here] = X[here] + v.reshape(shape)
-        if want_dir:
-            d = b * (flat(lev["IV"][here]) * r)
-            if a:
-                d = d + a * v
-            Vo[here] = d.reshape(shape)
+        v = [Vi[p - 1 + i] for i in range(g + 2)]
+        wx = [lev["WX"][p - 1 + i] for i in range(g + 1)]
+        for i in range(g):
+            c = v[i + 1]
+            wy, wz = lev["WY"][p + i], lev["WZ"][p + i]
+            total = wx[i + 1] * v[i + 2] + wx[i] * v[i]
+            total = total + (wy * up(c, 0) + down(wy * c, 0))
+            total = total + (wz * up(c, 1) + down(wz * c, 1))
+            r = R[p + i] - (lev["DG"][p + i] * c - total)
+            R[p + i] = r
+            own = c if part is None else c[part[0], part[1]]
+            X[p + i] = own if first else X[p + i] + own
+            if want_dir:
+                d = b * (lev["IV"][p + i] * r)
+                Vo[p + i] = d + a * c if a else d
 
     planes_loop(lo, hi, group, one)
 
 
-def presmooth(lev, R, X, halos, base, own, group, whole=False):
+def presmooth(lev, R, X, halos, base, own, group, whole=False, part=None, after=None):
     h = 0 if whole else halos[0] + 1
     lo, hi = base - h, base + own + h
 
@@ -141,20 +139,27 @@
         a, b = TABLE[j] if j < 3 else (0.0, 0.0)
         lo, hi = base - halos[j], base + own + halos[j]
         sweep(lev, R, X, names[j % 2], names[1 - j % 2], lo, hi, a, b, group,
-              first=(j == 0), want_dir=(j < 3))
-
-
-def postsmooth(lev, R, X, halos, base, own, group):
+              first=(j == 0), want_dir=(j < 3), part=part)
+        if after:
+            after(j)
+
+
+def postsmooth(lev, R, X, halos, base, own, group, part=None):
     names = ("Va", "Vb")
     for j in range(4):
         a, b = TABLE[j - 1] if j > 0 else (0.0, 1.0 / THETA)
         lo, hi = base - halos[j], base + own + halos[j]
-        sweep(lev, R, X, names[j % 2], names[1 - j % 2], lo, hi, a, b, group)
+        sweep(lev, R, X, names[j % 2], names[1 - j % 2], lo, hi, a, b, group, part=part)
 
 
 def kernel(sizes, names, *refs):
-    f_ref, k_ref, out_ref = refs[:3]
+    f_hbm, k_hbm, out_ref = refs[:3]
     S = dict(zip(names, refs[3:]))
+    f_ref, k_ref = S["FI"], S["KI"]
+    loads = [pltpu.make_async_copy(src, dst, S["ls"].at[i])
+             for i, (src, dst) in enumerate(((f_hbm, f_ref), (k_hbm, k_ref)))]
+    for c in loads:
+        c.start()
     ss, rs = S["ss"], S["rs"]
     NGX, NGY, NGZ = sizes
     NYC = NGY // 2
@@ -180,10 +185,16 @@
     barrier = pltpu.get_barrier_semaphore()
     greeted = [pair_dev(c, dz) for c, dz in pair_peers]
     greeted += [chip_dev(dy) for dy in range(1, NYC)]
-    greeted += [at(dx=d) for d in range(1, NGX)]
-    greeted += [at(dx=dx, dy=dy) for dx, dy in sides if dy != 0]
+    greeted += [at(dx=dx, dy=dy) for dx, dy in sides]
     for dev in greeted:
         pl.semaphore_signal(barrier, inc=1, device_id=dev, device_id_type=MESH)
+
+    def pass_on(i):
+        for d in (2 ** i, -(2 ** i)):
+            pl.semaphore_signal(S["dis"].at[i], inc=1, device_id=at(dx=d), device_id_type=MESH)
+
+    def heard(i):
+        pl.semaphore_wait(S["dis"].at[i], 2)
 
     counter = [0]
 
@@ -224,10 +235,11 @@
         out = []
         for d, n in ((1, n1), (2, n2)):
             if n:
-                out.append(remote(buf.at[:, pl.ds(11 - n, n)],
-                                  buf.at[:, pl.ds(7 - 4 * (d - 1) - n, n)], at(dx=d)))
-                out.append(remote(buf.at[:, pl.ds(7, n)],
-                                  buf.at[:, pl.ds(11 + 4 * (d - 1), n)], at(dx=-d)))
+                fld = slice(None) if d == 1 else slice(0, 1)
+                out.append(remote(buf.at[fld, pl.ds(11 - n, n)],
+                                  buf.at[fld, pl.ds(7 - 4 * (d - 1) - n, n)], at(dx=d)))
+                out.append(remote(buf.at[fld, pl.ds(7, n)],
+                                  buf.at[fld, pl.ds(11 + 4 * (d - 1), n)], at(dx=-d)))
         return out
 
     def pair_copies(buf, slots):
@@ -236,9 +248,6 @@
     def chip_copies(buf):
         mine = buf.at[0, pl.ds(7, 4), pl.ds(pl.multiple_of(chip * 8, 8), 8)]
         return [remote(mine, mine, chip_dev(dy)) for dy in range(1, NYC)]
-
-    def gather_copies(buf):
-        return [remote(buf.at[gx], buf.at[gx], at(dx=d)) for d in range(1, NGX)]
 
     lane16 = iota((16, 128), 1)
     lane8 = iota((8, 128), 1)
@@ -331,28 +340,29 @@
     F2, X2 = S["F2"].at[0], S["X2"]
     F3, X3 = S["F3"], S["X3"]
 
+    for c in loads:
+        c.wait()
     E0, E0r = S["E0"], S["E0r"]
     for fld, ref in ((0, f_ref), (1, k_ref)):
         for g, t in enumerate(pack0(lambda x: ref[x])):
             S["P0"][fld, g] = t
         body0(E0, fld, H0, ref)
-    k1 = coarse_0(k_ref[...].reshape(256, 128))
-    S["T1k"][0] = k1.reshape(8, 8, 128)
-    S["B2k"][...] = coarse_1(k1).reshape(4, 8, 128)
 
     pl.semaphore_wait(barrier, len(greeted))
     z0 = begin(z_copies(S["P0"], S["P0L"], S["P0R"]))
-    z1k = begin(z_copies(S["T1k"], S["T1kL"], S["T1kR"]))
-    p2k = begin(pair_copies(S["B2k"], S["B2kS"]))
-
+    pass_on(0)
     finish(z0)
     for fld in (0, 1):
         centre0(E0, fld, H0, None, S["P0L"], S["P0R"])
     xy0 = begin(xy_copies(E0, H0 + 1, 18, H0 + 1, 16))
-    finish(z1k)
-    centre1(S["K1"], 0, S["T1k"], S["T1kL"], S["T1kR"], 0)
-    xy1k = begin(xy_copies(S["K1"], 6, 8, H1K, 8))
-    finish(p2k)
+
+    k1 = coarse_0(k_ref[...].reshape(256, 128))
+    S["T1k"][0] = k1.reshape(8, 8, 128)
+    S["B2k"][...] = coarse_1(k1).reshape(4, 8, 128)
+    z1k = begin(z_copies(S["T1k"], S["T1kL"], S["T1kR"]))
+    p2k = begin(pair_copies(S["B2k"], S["B2kS"]))
+    heard(0)
+    pass_on(1)
 
     def pair_sum(own, slots):
         total = own[...]
@@ -361,13 +371,28 @@
         return total
 
     my_rows = pl.ds(pl.multiple_of(chip * 8, 8), 8)
-    if NYC * 8 < 32:
-        S["K2"][...] = jnp.zeros(S["K2"].shape, F32)
-        S["F2"][...] = jnp.zeros(S["F2"].shape, F32)
+    my_half = pl.ds(pl.multiple_of(core * 8, 8), 8)
+
+    def gather_start(v, buf):
+        S["C3"][...] = v
+        buf[gx, my_half] = S["C3"][my_half]
+        mine = buf.at[gx, my_half]
+        return begin([remote(mine, mine, at(dx=d)) for d in range(1, NGX)])
+
+    def swap_start(buf):
+        mine = buf.at[:, my_half]
+        return begin([remote(mine, mine, pair_dev(1, 0))])
+
+    finish(z1k)
+    centre1(S["K1"], 0, S["T1k"], S["T1kL"], S["T1kR"], 0)
+    finish(p2k)
     S["K2"][0, 7:11, my_rows] = pair_sum(S["B2k"], S["B2kS"])
+
+    finish(xy0)
+    xy1k = begin(xy_copies(S["K1"], 6, 8, H1K, 8))
     c2k = begin(chip_copies(S["K2"]))
-
-    finish(xy0)
+    heard(1)
+    pass_on(2)
 
     def lane0(l):
         return 128 * gz + jnp.where(l < 192, l, l - 256)
@@ -387,12 +412,16 @@
     unpack0(E0, 0, H0, -4, 20, put_r)
     weights(L0, 1, 25, 0.5, False, 1)
 
-    finish(c2k)
-    xx2k = begin(x_copies(S["K2"], 4, 3))
-    S["G3k"][gx] = coarse_2(S["K2"][0, 7:11].reshape(128, 128))
-    g3k = begin(gather_copies(S["G3k"]))
-
-    presmooth(L0, R0, X0, (3, 2, 1, 0), 5, 16, 1)
+    coef = {}
+
+    def after_sweep(j):
+        if j == 1:
+            finish(c2k)
+            coef["x"] = begin(x_copies(S["K2"], 4, 3))
+            heard(2)
+            coef["g"] = gather_start(coarse_2(S["K2"][0, 7:11].reshape(128, 128)), S["G3k"])
+
+    presmooth(L0, R0, X0, (3, 2, 1, 0), 5, 16, G0, part=OWN0, after=after_sweep)
 
     own0 = R0[5:21, 8:24, 0:128]
     S["T1f"][0] = coarse_0(own0.reshape(256, 128)).reshape(8, 8, 128)
@@ -400,8 +429,6 @@
     for g, t in enumerate(pack0(lambda x: R0[5 + x, 8:24, 0:128])):
         S["P0r"][0, g] = t
     E0r[0, H0R + 2:H0R + 18, 8:24] = own0
-    z0r = begin(z_copies(S["P0r"], S["P0rL"], S["P0rR"]))
-
     finish(xy1k)
 
     def lane1(l):
@@ -415,11 +442,12 @@
     finish(z1f)
     centre1(S["F1"], 0, S["T1f"], S["T1fL"], S["T1fR"], 0)
     xy1f = begin(xy_copies(S["F1"], 6, 8, H1F, 8))
+    z0r = begin(z_copies(S["P0r"], S["P0rL"], S["P0rR"]))
+    finish(xy1f)
     finish(z0r)
     centre0(E0r, 0, H0R, None, S["P0rL"], S["P0rR"])
     xy0r = begin(xy_copies(E0r, H0R + 1, 18, H0R + 1, 16))
-    finish(xy1f)
-    presmooth(L1, F1, X1, (3, 2, 1, 0), 6, 8, 2)
+    presmooth(L1, F1, X1, (3, 2, 1, 0), 6, 8, G1)
 
     r1 = F1[6:14, 8:16]
     S["B2f"][...] = coarse_1(r1.reshape(64, 128)).reshape(4, 8, 128)
@@ -428,7 +456,7 @@
     S["T1r"][1] = double1(X1[6:14, 8:16].reshape(64, 128)).reshape(8, 8, 128)
     z1r = begin(z_copies(S["T1r"], S["T1rL"], S["T1rR"]))
 
-    finish(xx2k)
+    finish(coef["x"])
     for p in range(18):
         if p < 7 or p > 10:
             L2["K"][p] = L2["K"][p] * xin(4 * gx + p - 7, NX1 // 2)
@@ -444,7 +472,8 @@
     xx2f = begin(x_copies(S["F2"], 4, 0))
     xy1r = begin(xy_copies(S["RX1"], 6, 8, H1R, 8))
 
-    finish(g3k)
+    finish(coef["g"])
+    finish(swap_start(S["G3k"]))
 
     def unpack3(slots, dst):
         for s in range(NGX):
@@ -460,10 +489,9 @@
     weights(L3, 5, 5 + NX3, 0.5 * 0.25 ** 3, True, 4)
 
     finish(xx2f)
-    presmooth(L2, F2, X2, (3, 2, 1, 0), 7, 4, 2)
-
-    S["G3f"][gx] = coarse_2(F2[7:11].reshape(128, 128))
-    g3f = begin(gather_copies(S["G3f"]))
+    presmooth(L2, F2, X2, (3, 2, 1, 0), 7, 4, G2)
+
+    g3f = gather_start(coarse_2(F2[7:11].reshape(128, 128)), S["G3f"])
     S["RX2"][0, 7:11] = F2[7:11]
     S["RX2"][1, 7:11] = X2[7:11]
     xx2r = begin(x_copies(S["RX2"], 4, 2))
@@ -486,8 +514,9 @@
     dg4 = h4 * (6.0 * k4 + ((k4xu + k4xd) + (k4yu + k4yd) + (k4zu + k4zd)))
 
     finish(g3f)
+    finish(swap_start(S["G3f"]))
     unpack3(S["G3f"], F3)
-    presmooth(L3, F3, X3, (0, 0, 0, 0), 5, NX3, 4, whole=True)
+    presmooth(L3, F3, X3, (0, 0, 0, 0), 5, NX3, G3, whole=True)
 
     f4 = coarse_3(F3[5:5 + NX3].reshape(16 * NX3, 128))
     f4 = jnp.where(k4 > 0.0, f4, 0.0)
@@ -508,7 +537,7 @@
         rr = rn
 
     L3["Va"][5:5 + NX3] = fine_3(x4).reshape(NX3, 16, 128)
-    postsmooth(L3, F3, X3, (0, 0, 0, 0), 5, NX3, 4)
+    postsmooth(L3, F3, X3, (0, 0, 0, 0), 5, NX3, G3)
     X3[5:5 + NX3] = X3[5:5 + NX3] + L3["Va"][5:5 + NX3]
 
     finish(xx2r)
@@ -521,7 +550,7 @@
             if 0 <= p < 18:
                 L2["Va"][p] = e
     R2b, X2b = S["RX2"].at[0], S["RX2"].at[1]
-    postsmooth(L2, R2b, X2b, (6, 5, 4, 3), 7, 4, 2)
+    postsmooth(L2, R2b, X2b, (6, 5, 4, 3), 7, 4, G2)
     X2b[4:14] = X2b[4:14] + L2["Va"][4:14]
 
     finish(xy1r)
@@ -538,7 +567,7 @@
         L1["Va"][2 * q] = e
         L1["Va"][2 * q + 1] = e
     R1b, X1b = S["RX1"].at[0], S["RX1"].at[1]
-    postsmooth(L1, R1b, X1b, (5, 4, 3, 2), 6, 8, 2)
+    postsmooth(L1, R1b, X1b, (5, 4, 3, 2), 6, 8, G1)
     X1b[4:16] = X1b[4:16] + L1["Va"][4:16]
 
     finish(xy0r)
@@ -561,19 +590,20 @@
         e = e * xin(8 * gx + q - 2, NX1)
         L0["Va"][1 + 2 * q] = e
         L0["Va"][2 + 2 * q] = e
-    postsmooth(L0, R0, X0, (3, 2, 1, 0), 5, 16, 1)
-    out_ref[...] = X0[5:21, 8:24, 0:128] + L0["Va"][5:21, 8:24, 0:128]
+    postsmooth(L0, R0, X0, (3, 2, 1, 0), 5, 16, G0, part=OWN0)
+    out_ref[...] = X0[5:21] + L0["Va"][5:21, 8:24, 0:128]
 
 
 def scratch(sizes):
     ngx, ngy, ngz = sizes
     n_pair = 2 * ngz - 1
     shapes = {
+        "FI": (16, 16, 128), "KI": (16, 16, 128), "C3": (16, 128),
         "P0": (2, 2, 16, 128), "P0L": (2, 2, 16, 128), "P0R": (2, 2, 16, 128),
         "E0": (2, 18 + 2 * (H0 + 1), 32, 128),
         "P0r": (1, 2, 16, 128), "P0rL": (1, 2, 16, 128), "P0rR": (1, 2, 16, 128),
         "E0r": (1, 18 + 2 * (H0R + 1), 32, 128),
-        "R0": (26, 32, 256), "X0": (26, 32, 256), "K0": (26, 32, 256),
+        "R0": (26, 32, 256), "X0": (26, 16, 128), "K0": (26, 32, 256),
         "T1r": (2, 8, 8, 128), "T1rL": (2, 8, 8, 128), "T1rR": (2, 8, 8, 128),
         "K1": (1, 20, 24, 128), "F1": (1, 20, 24, 128), "RX1": (2, 20, 24, 128), "X1": (20, 24, 128),
         "K2": (1, 18, 32, 128), "F2": (1, 18, 32, 128), "RX2": (2, 18, 32, 128), "X2": (18, 32, 128),
@@ -590,10 +620,11 @@
         shapes[n + "1"] = (20, 24, 128)
         shapes[n + "2"] = (18, 32, 128)
         shapes[n + "3"] = (2 * ngx + 10, 16, 128)
-    names = list(shapes) + ["ss", "rs"]
-    n_sem = 4 * 10 + 10 + 2 * (n_pair + max(ngy // 2 - 1, 0)) + 4 + 2 + 4 + 2 * (ngx - 1)
+    names = list(shapes) + ["ss", "rs", "ls", "dis"]
+    n_sem = 4 * 10 + 10 + 2 * (n_pair + max(ngy // 2 - 1, 0)) + 4 + 2 + 4 + 2 * ngx
     kinds = [pltpu.VMEM(shapes[n], F32) for n in shapes]
     kinds += [pltpu.SemaphoreType.DMA((n_sem,)), pltpu.SemaphoreType.DMA((n_sem,))]
+    kinds += [pltpu.SemaphoreType.DMA((2,)), pltpu.SemaphoreType.REGULAR((3,))]
     return names, kinds
 
 
@@ -606,7 +637,7 @@
         return pl.pallas_call(
             functools.partial(kernel, sizes, names),
             out_shape=jax.ShapeDtypeStruct(right_side.shape, F32),
-            in_specs=[pl.BlockSpec(memory_space=pltpu.VMEM)] * 2,
+            in_specs=[pl.BlockSpec(memory_space=pl.ANY)] * 2,
             out_specs=pl.BlockSpec(memory_space=pltpu.VMEM),
             scratch_shapes=kinds,
             compiler_params=pltpu.CompilerParams(

time: 100 us -> 81.4 us (0.81)
  the two profiles are of different devices: /device:TPU:2 before, /device:TPU:1 now
where the time goes in v2:
time: 81.4 us; the launch traced here: 81.2 us
  Pallas kernels  78.7 us (97%)
  local copies, waits for them, and re-layouts  2.47 us (3%)
    pallas_call x1, Pallas kernels, local(): pl.pallas_call(functools.partial(kernel, sizes, names), out_shape=jax.Sha...  78.7 us
    unnamed x5, local copies, waits for them, and re-layouts  2.47 us

profile of v2, /device:TPU:1, one launch (start us, length us, event | category | flops | bytes accessed | tf_op | source)
XLA Modules:
  0.0 81.2 jit_solution(2598477956064391761)
XLA Ops:
  0.0 0.0 copy-start
  0.0 0.9 %copy-done = f32[16,16,128]{2,1,0:T(8,128)S(1)} copy-done((f32[16,16,128]{2,1,0:T(8,128)S(1)}, f32[16,16,128]{2,1,0:T(8,128)}, u32[]{:S(2)}) %copy-start) | copy-done | bytes 131096
  0.9 0.0 copy-start.1
  0.9 0.9 %copy-done.1 = f32[16,16,128]{2,1,0:T(8,128)S(1)} copy-done((f32[16,16,128]{2,1,0:T(8,128)S(1)}, f32[16,16,128]{2,1,0:T(8,128)}, u32[]{:S(2)}) %copy-start.1) | copy-done | bytes 131096
  1.8 78.7 %shard_map.28 = f32[16,16,128]{2,1,0:T(8,128)S(1)} custom-call(f32[16,16,128]{2,1,0:T(8,128)S(1)} %copy-done, f32[16,16,128]{2,1,0:T(8,128)S(1)} %copy-done.1), custom_call_target="tpu_custom_call" | custom-call | tf_op jit(solution)/shard_map/pallas_call | solution.py:637
  80.6 0.7 copy.4
Async XLA Ops:
  0.0 0.9 %copy-start = (f32[16,16,128]{2,1,0:T(8,128)S(1)}, f32[16,16,128]{2,1,0:T(8,128)}, u32[]{:S(2)}) copy-start(f32[16,16,128]{2,1,0:T(8,128)} %refs_0_.1) | copy-start | bytes 393220
  0.9 0.9 %copy-start.1 = (f32[16,16,128]{2,1,0:T(8,128)S(1)}, f32[16,16,128]{2,1,0:T(8,128)}, u32[]{:S(2)}) copy-start(f32[16,16,128]{2,1,0:T(8,128)} %refs_1_.1) | copy-start | bytes 393220

commit v3 on v2

--- a/solution.py
+++ b/solution.py
@@ -16,7 +16,7 @@
 H0, H0R = 5, 3
 H1K, H1F, H1R = 6, 4, 5
 
-G0, G1, G2, G3 = 4, 8, 8, 16
+G0, G1, G2, G3 = 8, 20, 20, 32
 OWN0 = (slice(8, 24), slice(0, 128))
 
 
@@ -34,8 +34,27 @@
 TABLE = cheb_table()
 
 
-def mm(a, b):
-    return jnp.dot(a, b, precision=lax.Precision.HIGHEST, preferred_element_type=F32)
+def parts_of(v):
+    high = v.astype(jnp.bfloat16)
+    rest = v - high.astype(F32)
+    mid = rest.astype(jnp.bfloat16)
+    return high, mid, (rest - mid.astype(F32)).astype(jnp.bfloat16)
+
+
+def dot(a, b):
+    return jnp.dot(a, b, preferred_element_type=F32)
+
+
+def mml(m, v):
+    m = m.astype(jnp.bfloat16)
+    high, mid, low = parts_of(v)
+    return dot(m, high) + (dot(m, mid) + dot(m, low))
+
+
+def mmr(v, m):
+    m = m.astype(jnp.bfloat16)
+    high, mid, low = parts_of(v)
+    return dot(high, m) + (dot(mid, m) + dot(low, m))
 
 
 def iota(shape, dim):
@@ -155,9 +174,9 @@
 def kernel(sizes, names, *refs):
     f_hbm, k_hbm, out_ref = refs[:3]
     S = dict(zip(names, refs[3:]))
-    f_ref, k_ref = S["FI"], S["KI"]
-    loads = [pltpu.make_async_copy(src, dst, S["ls"].at[i])
-             for i, (src, dst) in enumerate(((f_hbm, f_ref), (k_hbm, k_ref)))]
+    E0 = S["E0"]
+    loads = [pltpu.make_async_copy(src, E0.at[i, pl.ds(H0, 16), pl.ds(8, 16)], S["ls"].at[i])
+             for i, src in enumerate((f_hbm, k_hbm))]
     for c in loads:
         c.start()
     ss, rs = S["ss"], S["rs"]
@@ -177,14 +196,14 @@
     def pair_dev(c, dz):
         return (gx, chip * 2 + (core + c) % 2, (gz + dz) % NGZ)
 
-    def chip_dev(dy):
-        return (gx, ((chip + dy) % NYC) * 2 + core, gz)
+    def chip_dev(dy, dx=0):
+        return ((gx + dx + NGX) % NGX, ((chip + dy) % NYC) * 2 + core, gz)
 
     sides = [(dx, dy) for dx in (-1, 0, 1) for dy in (-1, 0, 1) if (dx, dy) != (0, 0)]
 
     barrier = pltpu.get_barrier_semaphore()
     greeted = [pair_dev(c, dz) for c, dz in pair_peers]
-    greeted += [chip_dev(dy) for dy in range(1, NYC)]
+    greeted += [chip_dev(dy, dx) for dx in (-1, 0, 1) for dy in range(1, NYC)]
     greeted += [at(dx=dx, dy=dy) for dx, dy in sides]
     for dev in greeted:
         pl.semaphore_signal(barrier, inc=1, device_id=dev, device_id_type=MESH)
@@ -245,9 +264,12 @@
     def pair_copies(buf, slots):
         return [remote(buf, slots.at[i], pair_dev(c, dz)) for i, (c, dz) in enumerate(pair_peers)]
 
-    def chip_copies(buf):
-        mine = buf.at[0, pl.ds(7, 4), pl.ds(pl.multiple_of(chip * 8, 8), 8)]
-        return [remote(mine, mine, chip_dev(dy)) for dy in range(1, NYC)]
+    column = [(dx, dy) for dx in (-1, 0, 1) for dy in range(NYC) if (dx, dy) != (0, 0)]
+
+    def column_copies(buf):
+        rows = pl.ds(pl.multiple_of(chip * 8, 8), 8)
+        mine = buf.at[0, pl.ds(7, 4), rows]
+        return [remote(mine, buf.at[0, pl.ds(7 - 4 * dx, 4), rows], chip_dev(dy, dx)) for dx, dy in column]
 
     lane16 = iota((16, 128), 1)
     lane8 = iota((8, 128), 1)
@@ -258,30 +280,31 @@
     def coarse_0(r):
         c = sel((64, 256), lambda r, c: ((c >> 5) == (r >> 3)) & (((c & 15) >> 1) == (r & 7)), 0.25)
         z = sel((128, 128), lambda l, c: (l >> 1) == (c & 63), 0.5)
-        return mm(mm(c, r), z)
+        return mmr(mml(c, r), z)
 
     def coarse_1(r):
         c = sel((32, 64), lambda r, c: ((c >> 4) == (r >> 3)) & (((c & 7) >> 1) == (r & 7) - 4 * core), 0.25)
-        z = sel((128, 128), lambda l, c: (l < 64) & (c == 32 * gz + (l >> 1)), 0.5)
-        return mm(mm(c, r), z)
+        z = sel((128, 128), lambda l, c: (l < 64) & (c == (l >> 1)), 0.5)
+        t = mmr(mml(c, r), z)
+        return (t[0:8] + pltpu.roll(t[8:16], 32, 1)) + (pltpu.roll(t[16:24], 64, 1) + pltpu.roll(t[24:32], 96, 1))
 
     def coarse_2(r):
         c = sel((32, 128), lambda r, c: ((c >> 6) == (r >> 4)) & (((c & 31) >> 1) == (r & 15)), 0.25)
         z = sel((128, 128), lambda l, c: (l >> 1) == (c & 63), 0.5)
-        t = mm(mm(c, r), z)
+        t = mmr(mml(c, r), z)
         return jnp.where(lane16 < 64, t[0:16], t[16:32])
 
     def coarse_3(r):
         n = r.shape[0]
         c = sel((n // 4, n), lambda r, c: ((c >> 5) == (r >> 3)) & (((c & 15) >> 1) == (r & 7)), 0.25)
         z = sel((128, 128), lambda l, c: (l < 64) & ((l >> 1) == c), 0.5)
-        return mm(mm(c, r), z)
+        return mmr(mml(c, r), z)
 
     def fine_3(e):
         n = e.shape[0]
         u = sel((4 * n, n), lambda r, c: ((r >> 5) == (c >> 3)) & (((r & 15) >> 1) == (c & 7)), 1.0)
         z = sel((128, 128), lambda c, l: (l < 64) & ((l >> 1) == c), 1.0)
-        return mm(u, mm(e, z))
+        return mml(u, mmr(e, z))
 
     def pack0(field):
         out = []
@@ -293,14 +316,17 @@
             out.append(acc)
         return out
 
-    def centre0(buf, fld, h, field, from_left, from_right):
-        base = h + 1
-        for g, m in ((0, base), (1, base + 17)):
-            buf[fld, m, 8:24] = jnp.where((lane16 & 15) >= 8, from_right[fld, g], from_left[fld, g])
-
-    def body0(buf, fld, h, ref):
-        base = h + 1
-        buf[fld, base + 1:base + 17, 8:24] = ref[...]
+    def merge0(from_left, from_right):
+        return jnp.where((lane16 & 15) >= 8, from_right, from_left)
+
+    def centre0(buf, fld, h, from_left, from_right):
+        for g, m in ((0, h + 1), (1, h + 18)):
+            buf[fld, m, 8:24] = merge0(from_left[fld, g], from_right[fld, g])
+
+    def open0(fld, lo, hi, put):
+        for x in range(lo, hi):
+            g, j = (x + 8) // 8, x % 8
+            put(x, E0[fld, H0 + x], pltpu.roll(M0[fld, g], (120 - 16 * j) % 128, 1))
 
     def unpack0(buf, fld, h, lo, hi, put):
         for x in range(lo, hi):
@@ -311,6 +337,24 @@
             else:
                 main, m, j = h + 20 + x - 16, h + 19, x - 16
             put(x, buf[fld, main], pltpu.roll(buf[fld, m], (120 - 16 * j) % 128, 1))
+
+    def pack1(v):
+        acc = None
+        for j in range(8):
+            t = v[8 * j:8 * j + 8]
+            low = pltpu.roll(t, 8 * j, 1) if j else t
+            high = pltpu.roll(t, 8 * j + 8, 1)
+            acc = low if acc is None else jnp.where((lane8 >> 3) == j, low, acc)
+            acc = jnp.where((lane8 >> 3) == 8 + j, high, acc)
+        return acc
+
+    def corner_copies(pack, from_left, from_right):
+        out = []
+        for dz, buf in ((1, from_left), (-1, from_right)):
+            for dx in (-1, 0, 1):
+                for dy in (-1, 0, 1):
+                    out.append(remote(pack, buf.at[pl.ds(1 - dx, 1), pl.ds(8 - 8 * dy, 8)], at(dx, dy, dz)))
+        return out
 
     def double1(v):
         n = v.shape[0]
@@ -342,33 +386,45 @@
 
     for c in loads:
         c.wait()
-    E0, E0r = S["E0"], S["E0r"]
-    for fld, ref in ((0, f_ref), (1, k_ref)):
-        for g, t in enumerate(pack0(lambda x: ref[x])):
+    E0r, M0 = S["E0r"], S["M0"]
+    pl.semaphore_wait(barrier, len(greeted))
+    xy0 = begin(xy_copies(E0, H0, 16, H0, 16))
+    for fld in (0, 1):
+        for g, t in enumerate(pack0(lambda x: E0[fld, H0 + x, 8:24])):
             S["P0"][fld, g] = t
-        body0(E0, fld, H0, ref)
-
-    pl.semaphore_wait(barrier, len(greeted))
     z0 = begin(z_copies(S["P0"], S["P0L"], S["P0R"]))
     pass_on(0)
     finish(z0)
     for fld in (0, 1):
-        centre0(E0, fld, H0, None, S["P0L"], S["P0R"])
-    xy0 = begin(xy_copies(E0, H0 + 1, 18, H0 + 1, 16))
-
-    k1 = coarse_0(k_ref[...].reshape(256, 128))
+        for g in (0, 1):
+            M0[fld, 1 + g, 8:24] = merge0(S["P0L"][fld, g], S["P0R"][fld, g])
+    xy0 += begin(xy_copies(M0, 1, 2, 1, 16))
+
+    k1 = coarse_0(E0[1, H0:H0 + 16, 8:24].reshape(256, 128))
     S["T1k"][0] = k1.reshape(8, 8, 128)
-    S["B2k"][...] = coarse_1(k1).reshape(4, 8, 128)
+    S["B2k"][...] = coarse_1(k1)
     z1k = begin(z_copies(S["T1k"], S["T1kL"], S["T1kR"]))
     p2k = begin(pair_copies(S["B2k"], S["B2kS"]))
     heard(0)
     pass_on(1)
 
-    def pair_sum(own, slots):
-        total = own[...]
-        for i in range(len(pair_peers)):
-            total = total + slots[i]
-        return total
+    def pair_rows(own, slots):
+        blocks = [[] for _ in range(NGZ)]
+        blocks[0].append(own[...])
+        for i, (_, dz) in enumerate(pair_peers):
+            blocks[dz].append(slots[i])
+        rows = [jnp.zeros((8, 128), F32)] * 4
+        for dz in range(NGZ):
+            g = (gz - dz + NGZ) % NGZ
+            t = pltpu.roll(sum(blocks[dz][1:], blocks[dz][0]), 32 * g, 1)
+            here = (lane8 >> 5) == g
+            for x in range(4):
+                rows[x] = jnp.where(here, t if x == 0 else pltpu.roll(t, 128 - 32 * x, 1), rows[x])
+        return rows
+
+    def put_rows(buf, rows):
+        for x in range(4):
+            buf[0, 7 + x, my_rows] = rows[x]
 
     my_rows = pl.ds(pl.multiple_of(chip * 8, 8), 8)
     my_half = pl.ds(pl.multiple_of(core * 8, 8), 8)
@@ -386,11 +442,11 @@
     finish(z1k)
     centre1(S["K1"], 0, S["T1k"], S["T1kL"], S["T1kR"], 0)
     finish(p2k)
-    S["K2"][0, 7:11, my_rows] = pair_sum(S["B2k"], S["B2kS"])
+    put_rows(S["K2"], pair_rows(S["B2k"], S["B2kS"]))
 
     finish(xy0)
     xy1k = begin(xy_copies(S["K1"], 6, 8, H1K, 8))
-    c2k = begin(chip_copies(S["K2"]))
+    c2k = begin(column_copies(S["K2"]))
     heard(1)
     pass_on(2)
 
@@ -408,27 +464,22 @@
         R0[x + 5, :, 0:128] = main
         R0[x + 5, :, 128:256] = halo
 
-    unpack0(E0, 1, H0, -5, 21, put_k)
-    unpack0(E0, 0, H0, -4, 20, put_r)
+    open0(1, -5, 21, put_k)
+    open0(0, -4, 20, put_r)
     weights(L0, 1, 25, 0.5, False, 1)
 
-    coef = {}
-
-    def after_sweep(j):
-        if j == 1:
-            finish(c2k)
-            coef["x"] = begin(x_copies(S["K2"], 4, 3))
-            heard(2)
-            coef["g"] = gather_start(coarse_2(S["K2"][0, 7:11].reshape(128, 128)), S["G3k"])
-
-    presmooth(L0, R0, X0, (3, 2, 1, 0), 5, 16, G0, part=OWN0, after=after_sweep)
+    presmooth(L0, R0, X0, (3, 2, 1, 0), 5, 16, G0, part=OWN0)
 
     own0 = R0[5:21, 8:24, 0:128]
-    S["T1f"][0] = coarse_0(own0.reshape(256, 128)).reshape(8, 8, 128)
-    z1f = begin(z_copies(S["T1f"], S["T1fL"], S["T1fR"]))
+    f1 = coarse_0(own0.reshape(256, 128))
+    S["F1"][0, 6:14, 8:16] = f1.reshape(8, 8, 128)
+    S["P1"][0] = pack1(f1)
+    xy1f = begin(xy_copies(S["F1"], 6, 8, H1F, 8) + corner_copies(S["P1"], S["Z1L"], S["Z1R"]))
     for g, t in enumerate(pack0(lambda x: R0[5 + x, 8:24, 0:128])):
         S["P0r"][0, g] = t
     E0r[0, H0R + 2:H0R + 18, 8:24] = own0
+    finish(c2k)
+    xx2k = begin(x_copies(S["K2"], 0, 3))
     finish(xy1k)
 
     def lane1(l):
@@ -439,40 +490,50 @@
         L1["K"][p] = L1["K"][p] * (in1 * xin(8 * gx + p - 6, NX1))
     weights(L1, 1, 19, 0.5 * 0.25, False, 2)
 
-    finish(z1f)
-    centre1(S["F1"], 0, S["T1f"], S["T1fL"], S["T1fR"], 0)
-    xy1f = begin(xy_copies(S["F1"], 6, 8, H1F, 8))
     z0r = begin(z_copies(S["P0r"], S["P0rL"], S["P0rR"]))
     finish(xy1f)
+    edges = [jnp.where(iota((24, 128), 1) < 64, S["Z1R"][g], S["Z1L"][g]) for g in range(3)]
+    lane24 = iota((24, 128), 1)
+    for x in range(-H1F, 8 + H1F):
+        g, j = (x + 8) // 8, x % 8
+        right = pltpu.roll(edges[g], (64 - 8 * j) % 128, 1)
+        left = pltpu.roll(edges[g], (56 - 8 * j) % 128, 1)
+        F1[6 + x] = jnp.where(lane24 < 64, F1[6 + x], jnp.where(lane24 < 96, right, left))
     finish(z0r)
-    centre0(E0r, 0, H0R, None, S["P0rL"], S["P0rR"])
+    centre0(E0r, 0, H0R, S["P0rL"], S["P0rR"])
     xy0r = begin(xy_copies(E0r, H0R + 1, 18, H0R + 1, 16))
+    heard(2)
+    g3k = gather_start(coarse_2(S["K2"][0, 7:11].reshape(128, 128)), S["G3k"])
     presmooth(L1, F1, X1, (3, 2, 1, 0), 6, 8, G1)
 
     r1 = F1[6:14, 8:16]
-    S["B2f"][...] = coarse_1(r1.reshape(64, 128)).reshape(4, 8, 128)
+    S["B2f"][...] = coarse_1(r1.reshape(64, 128))
     p2f = begin(pair_copies(S["B2f"], S["B2fS"]))
     S["T1r"][0] = double1(r1.reshape(64, 128)).reshape(8, 8, 128)
     S["T1r"][1] = double1(X1[6:14, 8:16].reshape(64, 128)).reshape(8, 8, 128)
     z1r = begin(z_copies(S["T1r"], S["T1rL"], S["T1rR"]))
 
-    finish(coef["x"])
+    finish(xx2k)
     for p in range(18):
         if p < 7 or p > 10:
             L2["K"][p] = L2["K"][p] * xin(4 * gx + p - 7, NX1 // 2)
     weights(L2, 1, 17, 0.5 * 0.25 ** 2, True, 2)
 
     finish(p2f)
-    S["F2"][0, 7:11, my_rows] = pair_sum(S["B2f"], S["B2fS"])
-    c2f = begin(chip_copies(S["F2"]))
+    put_rows(S["F2"], pair_rows(S["B2f"], S["B2fS"]))
+    c2f = begin(column_copies(S["F2"]))
     finish(z1r)
     for i in (0, 1):
         centre1(S["RX1"], i, S["T1r"], S["T1rL"], S["T1rR"], i)
+
     finish(c2f)
-    xx2f = begin(x_copies(S["F2"], 4, 0))
-    xy1r = begin(xy_copies(S["RX1"], 6, 8, H1R, 8))
-
-    finish(coef["g"])
+    presmooth(L2, F2, X2, (3, 2, 1, 0), 7, 4, G2)
+
+    g3f = gather_start(coarse_2(F2[7:11].reshape(128, 128)), S["G3f"])
+    S["RX2"][0, 7:11] = F2[7:11]
+    S["RX2"][1, 7:11] = X2[7:11]
+
+    finish(g3k)
     finish(swap_start(S["G3k"]))
 
     def unpack3(slots, dst):
@@ -488,64 +549,81 @@
         ref[5 + NX3:10 + NX3] = zero3
     weights(L3, 5, 5 + NX3, 0.5 * 0.25 ** 3, True, 4)
 
-    finish(xx2f)
-    presmooth(L2, F2, X2, (3, 2, 1, 0), 7, 4, G2)
-
-    g3f = gather_start(coarse_2(F2[7:11].reshape(128, 128)), S["G3f"])
-    S["RX2"][0, 7:11] = F2[7:11]
-    S["RX2"][1, 7:11] = X2[7:11]
-    xx2r = begin(x_copies(S["RX2"], 4, 2))
-
-    n4 = 8 * (NX3 // 2)
+
+    def compact4(v):
+        v = v.reshape(4, 32, 128)
+        return (v[0] + pltpu.roll(v[1], 32, 1)) + (pltpu.roll(v[2], 64, 1) + pltpu.roll(v[3], 96, 1))
+
+    def spread4(v):
+        return jnp.concatenate([v] + [pltpu.roll(v, 128 - 32 * c, 1) for c in (1, 2, 3)], axis=0)
+
     h4 = 0.5 * 0.25 ** 4
     k4 = coarse_3(L3["K"][5:5 + NX3].reshape(16 * NX3, 128))
-    row4 = iota((n4, 128), 0)
-    plane_end = (row4 & 7) == 7
-    last_plane = row4 >= n4 - 8
-    first_plane = row4 < 8
-    k4xu = jnp.where(last_plane, 0.0, up(k4, 0, 8))
-    k4xd = jnp.where(first_plane, 0.0, down(k4, 0, 8))
-    k4yu = jnp.where(plane_end, 0.0, up(k4, 0))
-    k4yd = jnp.where((row4 & 7) == 0, 0.0, down(k4, 0))
-    k4zu, k4zd = up(k4, 1), down(k4, 1)
-    wx4 = jnp.where(last_plane, 0.0, h4 * (k4 + k4xu))
-    wy4 = jnp.where(plane_end, 0.0, h4 * (k4 + k4yu))
-    wz4 = h4 * (k4 + k4zu)
+    k4 = compact4(k4)
+    row4, lane4 = iota((32, 128), 0), iota((32, 128), 1)
+    x_first, x_last = (row4 < 8) & (lane4 < 32), (row4 >= 24) & (lane4 >= 96)
+    y_first, y_last = (row4 & 7) == 0, (row4 & 7) == 7
+    z_first, z_last = (lane4 & 31) == 0, (lane4 & 31) == 31
+
+    def xup(v):
+        return jnp.concatenate([v[8:32], pltpu.roll(v[0:8], 96, 1)], axis=0)
+
+    def xdown(v):
+        return jnp.concatenate([pltpu.roll(v[24:32], 32, 1), v[0:24]], axis=0)
+
+    k4xu, k4xd = jnp.where(x_last, 0.0, xup(k4)), jnp.where(x_first, 0.0, xdown(k4))
+    k4yu, k4yd = jnp.where(y_last, 0.0, up(k4, 0)), jnp.where(y_first, 0.0, down(k4, 0))
+    k4zu, k4zd = jnp.where(z_last, 0.0, up(k4, 1)), jnp.where(z_first, 0.0, down(k4, 1))
+    wx4 = jnp.where(x_last, 0.0, h4 * (k4 + k4xu))
+    wy4 = jnp.where(y_last, 0.0, h4 * (k4 + k4yu))
+    wz4 = jnp.where(z_last, 0.0, h4 * (k4 + k4zu))
     dg4 = h4 * (6.0 * k4 + ((k4xu + k4xd) + (k4yu + k4yd) + (k4zu + k4zd)))
 
     finish(g3f)
+    xx2r = begin(x_copies(S["RX2"], 4, 2))
+    xy1r = begin(xy_copies(S["RX1"], 6, 8, H1R, 8))
     finish(swap_start(S["G3f"]))
     unpack3(S["G3f"], F3)
     presmooth(L3, F3, X3, (0, 0, 0, 0), 5, NX3, G3, whole=True)
 
     f4 = coarse_3(F3[5:5 + NX3].reshape(16 * NX3, 128))
-    f4 = jnp.where(k4 > 0.0, f4, 0.0)
+    f4 = compact4(f4)
     x4 = jnp.zeros_like(f4)
     r4 = p4 = f4
-    rr = jnp.sum(r4 * r4, keepdims=True)
+
+    def total4(v):
+        t = (v[0:8] + v[8:16]) + (v[16:24] + v[24:32])
+        t = jnp.broadcast_to(jnp.sum(t, axis=1, keepdims=True), (8, 128))
+        for step in (4, 2, 1):
+            t = t + pltpu.roll(t, step, 0)
+        return t
+
+    def times4(c, v):
+        return (c[None] * v.reshape(4, 8, 128)).reshape(32, 128)
+
+    rr = total4(r4 * r4)
     for _ in range(CG_ITERS):
         q4 = dg4 * p4 - (
-            (wx4 * up(p4, 0, 8) + down(wx4 * p4, 0, 8))
+            (wx4 * xup(p4) + xdown(wx4 * p4))
             + (wy4 * up(p4, 0) + down(wy4 * p4, 0))
             + (wz4 * up(p4, 1) + down(wz4 * p4, 1)))
-        q4 = jnp.where(k4 > 0.0, q4, 0.0)
-        alpha = rr / jnp.sum(p4 * q4, keepdims=True)
-        x4 = x4 + alpha * p4
-        r4 = r4 - alpha * q4
-        rn = jnp.sum(r4 * r4, keepdims=True)
-        p4 = r4 + (rn / rr) * p4
+        alpha = rr / total4(p4 * q4)
+        x4 = x4 + times4(alpha, p4)
+        r4 = r4 - times4(alpha, q4)
+        rn = total4(r4 * r4)
+        p4 = r4 + times4(rn / rr, p4)
         rr = rn
 
-    L3["Va"][5:5 + NX3] = fine_3(x4).reshape(NX3, 16, 128)
+    L3["Va"][5:5 + NX3] = fine_3(spread4(x4)).reshape(NX3, 16, 128)
     postsmooth(L3, F3, X3, (0, 0, 0, 0), 5, NX3, G3)
     X3[5:5 + NX3] = X3[5:5 + NX3] + L3["Va"][5:5 + NX3]
 
     finish(xx2r)
     z3 = sel((128, 128), lambda c, l: (l >> 1) == c, 1.0)
     y3 = sel((32, 16), lambda r, c: (r >> 1) == c, 1.0)
-    t = mm(X3[pl.ds(2 * gx + 1, 10)].reshape(160, 128), z3)
+    t = mmr(X3[pl.ds(2 * gx + 1, 10)].reshape(160, 128), z3)
     for q in range(10):
-        e = mm(y3, t[16 * q:16 * q + 16])
+        e = mml(y3, t[16 * q:16 * q + 16])
         for p in (2 * q - 1, 2 * q):
             if 0 <= p < 18:
                 L2["Va"][p] = e
@@ -560,9 +638,9 @@
         return 8 * gy + r - 8
 
     y2 = sel((24, 32), lambda r, c: ((yrow(r) >> 1) == c) & (yrow(r) >= 0) & (yrow(r) < NY1), 1.0)
-    t = mm(X2b[4:14].reshape(320, 128), z2)
+    t = mmr(X2b[4:14].reshape(320, 128), z2)
     for q in range(10):
-        e = mm(y2, t[32 * q:32 * q + 32])
+        e = mml(y2, t[32 * q:32 * q + 32])
         e = e * xin(4 * gx + q - 3, NX1 // 2)
         L1["Va"][2 * q] = e
         L1["Va"][2 * q + 1] = e
@@ -584,9 +662,9 @@
 
     z1 = sel((128, 256), zfine, 1.0)
     y1 = sel((32, 24), yfine, 1.0)
-    t = mm(X1b[4:16].reshape(288, 128), z1)
+    t = mmr(X1b[4:16].reshape(288, 128), z1)
     for q in range(12):
-        e = mm(y1, t[24 * q:24 * q + 24])
+        e = mml(y1, t[24 * q:24 * q + 24])
         e = e * xin(8 * gx + q - 2, NX1)
         L0["Va"][1 + 2 * q] = e
         L0["Va"][2 + 2 * q] = e
@@ -598,17 +676,18 @@
     ngx, ngy, ngz = sizes
     n_pair = 2 * ngz - 1
     shapes = {
-        "FI": (16, 16, 128), "KI": (16, 16, 128), "C3": (16, 128),
+        "C3": (16, 128), "M0": (2, 4, 32, 128),
+        "P1": (1, 8, 128), "Z1L": (3, 24, 128), "Z1R": (3, 24, 128),
         "P0": (2, 2, 16, 128), "P0L": (2, 2, 16, 128), "P0R": (2, 2, 16, 128),
-        "E0": (2, 18 + 2 * (H0 + 1), 32, 128),
+        "E0": (2, 16 + 2 * H0, 32, 128),
         "P0r": (1, 2, 16, 128), "P0rL": (1, 2, 16, 128), "P0rR": (1, 2, 16, 128),
         "E0r": (1, 18 + 2 * (H0R + 1), 32, 128),
         "R0": (26, 32, 256), "X0": (26, 16, 128), "K0": (26, 32, 256),
         "T1r": (2, 8, 8, 128), "T1rL": (2, 8, 8, 128), "T1rR": (2, 8, 8, 128),
         "K1": (1, 20, 24, 128), "F1": (1, 20, 24, 128), "RX1": (2, 20, 24, 128), "X1": (20, 24, 128),
         "K2": (1, 18, 32, 128), "F2": (1, 18, 32, 128), "RX2": (2, 18, 32, 128), "X2": (18, 32, 128),
-        "B2k": (4, 8, 128), "B2kS": (n_pair, 4, 8, 128),
-        "B2f": (4, 8, 128), "B2fS": (n_pair, 4, 8, 128),
+        "B2k": (8, 128), "B2kS": (n_pair, 8, 128),
+        "B2f": (8, 128), "B2fS": (n_pair, 8, 128),
         "G3k": (ngx, 16, 128), "G3f": (ngx, 16, 128),
         "K3": (2 * ngx + 10, 16, 128), "F3": (2 * ngx + 10, 16, 128), "X3": (2 * ngx + 10, 16, 128),
     }
@@ -621,7 +700,7 @@
         shapes[n + "2"] = (18, 32, 128)
         shapes[n + "3"] = (2 * ngx + 10, 16, 128)
     names = list(shapes) + ["ss", "rs", "ls", "dis"]
-    n_sem = 4 * 10 + 10 + 2 * (n_pair + max(ngy // 2 - 1, 0)) + 4 + 2 + 4 + 2 * ngx
+    n_sem = 74 + 2 * (n_pair + 3 * (ngy // 2) - 1) + 2 + 4 + 2 * ngx
     kinds = [pltpu.VMEM(shapes[n], F32) for n in shapes]
     kinds += [pltpu.SemaphoreType.DMA((n_sem,)), pltpu.SemaphoreType.DMA((n_sem,))]
     kinds += [pltpu.SemaphoreType.DMA((2,)), pltpu.SemaphoreType.REGULAR((3,))]

time: 81.4 us -> 72.2 us (0.89)
  Pallas kernels: 78.7 us -> 69.6 us
    pallas_call x1, Pallas kernels: 78.7 us -> 69.6 us  [local(): pl.pallas_call(functools.partial(kernel, sizes, names), out_shape=jax.Sha...]
where the time goes in v3:
time: 72.2 us; the launch traced here: 72 us
  Pallas kernels  69.6 us (96%)
  local copies, waits for them, and re-layouts  2.47 us (3%)
    pallas_call x1, Pallas kernels, local(): pl.pallas_call(functools.partial(kernel, sizes, names), out_shape=jax.Sha...  69.6 us
    unnamed x5, local copies, waits for them, and re-layouts  2.47 us

profile of v3, /device:TPU:1, one launch (start us, length us, event | category | flops | bytes accessed | tf_op | source)
XLA Modules:
  0.0 72.0 jit_solution(1187735284468845004)
XLA Ops:
  0.0 0.0 copy-start
  0.0 0.9 %copy-done = f32[16,16,128]{2,1,0:T(8,128)S(1)} copy-done((f32[16,16,128]{2,1,0:T(8,128)S(1)}, f32[16,16,128]{2,1,0:T(8,128)}, u32[]{:S(2)}) %copy-start) | copy-done | bytes 131096
  0.9 0.0 copy-start.1
  0.9 0.9 %copy-done.1 = f32[16,16,128]{2,1,0:T(8,128)S(1)} copy-done((f32[16,16,128]{2,1,0:T(8,128)S(1)}, f32[16,16,128]{2,1,0:T(8,128)}, u32[]{:S(2)}) %copy-start.1) | copy-done | bytes 131096
  1.8 69.6 %shard_map.28 = f32[16,16,128]{2,1,0:T(8,128)S(1)} custom-call(f32[16,16,128]{2,1,0:T(8,128)S(1)} %copy-done, f32[16,16,128]{2,1,0:T(8,128)S(1)} %copy-done.1), custom_call_target="tpu_custom_call" | custom-call | tf_op jit(solution)/shard_map/pallas_call | solution.py:716
  71.4 0.7 copy.4
Async XLA Ops:
  0.0 0.9 %copy-start = (f32[16,16,128]{2,1,0:T(8,128)S(1)}, f32[16,16,128]{2,1,0:T(8,128)}, u32[]{:S(2)}) copy-start(f32[16,16,128]{2,1,0:T(8,128)} %refs_0_.1) | copy-start | bytes 393220
  0.9 0.9 %copy-start.1 = (f32[16,16,128]{2,1,0:T(8,128)S(1)}, f32[16,16,128]{2,1,0:T(8,128)}, u32[]{:S(2)}) copy-start(f32[16,16,128]{2,1,0:T(8,128)} %refs_1_.1) | copy-start | bytes 393220

commit v4 on v3

--- a/solution.py
+++ b/solution.py
@@ -121,7 +121,8 @@
     planes_loop(lo, hi, group, one)
 
 
-def sweep(lev, R, X, src, dst, lo, hi, a, b, group, first=False, want_dir=True, part=None):
+def sweep(lev, R, X, src, dst, lo, hi, a, b, group, first=False, want_dir=True, part=None,
+          fold=False, out=None):
     Vi, Vo = lev[src], lev[dst]
 
     def one(p, g):
@@ -134,12 +135,20 @@
             total = total + (wy * up(c, 0) + down(wy * c, 0))
             total = total + (wz * up(c, 1) + down(wz * c, 1))
             r = R[p + i] - (lev["DG"][p + i] * c - total)
-            R[p + i] = r
-            own = c if part is None else c[part[0], part[1]]
-            X[p + i] = own if first else X[p + i] + own
             if want_dir:
                 d = b * (lev["IV"][p + i] * r)
-                Vo[p + i] = d + a * c if a else d
+                d = d + a * c if a else d
+            step = c + d if fold else c
+            own = step if part is None else step[part[0], part[1]]
+            x = own if first else X[p + i] + own
+            if out is None:
+                X[p + i] = x
+            else:
+                out[p + i - lo] = x
+            if not fold:
+                R[p + i] = r
+            if want_dir and not fold:
+                Vo[p + i] = d
 
     planes_loop(lo, hi, group, one)
 
@@ -163,12 +172,13 @@
             after(j)
 
 
-def postsmooth(lev, R, X, halos, base, own, group, part=None):
+def postsmooth(lev, R, X, halos, base, own, group, part=None, out=None):
     names = ("Va", "Vb")
     for j in range(4):
         a, b = TABLE[j - 1] if j > 0 else (0.0, 1.0 / THETA)
         lo, hi = base - halos[j], base + own + halos[j]
-        sweep(lev, R, X, names[j % 2], names[1 - j % 2], lo, hi, a, b, group, part=part)
+        sweep(lev, R, X, names[j % 2], names[1 - j % 2], lo, hi, a, b, group, part=part,
+              fold=(j == 3), out=out if j == 3 else None)
 
 
 def kernel(sizes, names, *refs):
@@ -387,12 +397,12 @@
     for c in loads:
         c.wait()
     E0r, M0 = S["E0r"], S["M0"]
-    pl.semaphore_wait(barrier, len(greeted))
-    xy0 = begin(xy_copies(E0, H0, 16, H0, 16))
     for fld in (0, 1):
         for g, t in enumerate(pack0(lambda x: E0[fld, H0 + x, 8:24])):
             S["P0"][fld, g] = t
+    pl.semaphore_wait(barrier, len(greeted))
     z0 = begin(z_copies(S["P0"], S["P0L"], S["P0R"]))
+    xy0 = begin(xy_copies(E0, H0, 16, H0, 16))
     pass_on(0)
     finish(z0)
     for fld in (0, 1):
@@ -616,7 +626,6 @@
 
     L3["Va"][5:5 + NX3] = fine_3(spread4(x4)).reshape(NX3, 16, 128)
     postsmooth(L3, F3, X3, (0, 0, 0, 0), 5, NX3, G3)
-    X3[5:5 + NX3] = X3[5:5 + NX3] + L3["Va"][5:5 + NX3]
 
     finish(xx2r)
     z3 = sel((128, 128), lambda c, l: (l >> 1) == c, 1.0)
@@ -629,7 +638,6 @@
                 L2["Va"][p] = e
     R2b, X2b = S["RX2"].at[0], S["RX2"].at[1]
     postsmooth(L2, R2b, X2b, (6, 5, 4, 3), 7, 4, G2)
-    X2b[4:14] = X2b[4:14] + L2["Va"][4:14]
 
     finish(xy1r)
     z2 = sel((128, 128), lambda c, l: ((lane1(l) >> 1) == c) & (lane1(l) >= 0) & (lane1(l) < NZ1), 1.0)
@@ -646,7 +654,6 @@
         L1["Va"][2 * q + 1] = e
     R1b, X1b = S["RX1"].at[0], S["RX1"].at[1]
     postsmooth(L1, R1b, X1b, (5, 4, 3, 2), 6, 8, G1)
-    X1b[4:16] = X1b[4:16] + L1["Va"][4:16]
 
     finish(xy0r)
     unpack0(E0r, 0, H0R, -3, 19, put_r)
@@ -668,8 +675,7 @@
         e = e * xin(8 * gx + q - 2, NX1)
         L0["Va"][1 + 2 * q] = e
         L0["Va"][2 + 2 * q] = e
-    postsmooth(L0, R0, X0, (3, 2, 1, 0), 5, 16, G0, part=OWN0)
-    out_ref[...] = X0[5:21] + L0["Va"][5:21, 8:24, 0:128]
+    postsmooth(L0, R0, X0, (3, 2, 1, 0), 5, 16, G0, part=OWN0, out=out_ref)
 
 
 def scratch(sizes):
@@ -720,7 +726,7 @@
             out_specs=pl.BlockSpec(memory_space=pltpu.VMEM),
             scratch_shapes=kinds,
             compiler_params=pltpu.CompilerParams(
-                collective_id=0, has_side_effects=True, vmem_limit_bytes=48 * 1024 * 1024
+                collective_id=0, has_side_effects=True, vmem_limit_bytes=57 * 1024 * 1024
             ),
         )(right_side, conductivity)
 

time: 72.2 us -> 71.6 us (level)
  local copies, waits for them, and re-layouts: 2.47 us -> 1.57 us
    unnamed x5 -> x1, local copies, waits for them, and re-layouts: 2.47 us -> 1.57 us
where the time goes in v4:
time: 71.6 us; the launch traced here: 71.5 us
  Pallas kernels  69.9 us (98%)
  local copies, waits for them, and re-layouts  1.57 us (2%)
    pallas_call x1, Pallas kernels, local(): pl.pallas_call(functools.partial(kernel, sizes, names), out_shape=jax.Sha...  69.9 us
    unnamed x1, local copies, waits for them, and re-layouts  1.57 us

profile of v4, /device:TPU:1, one launch (start us, length us, event | category | flops | bytes accessed | tf_op | source)
XLA Modules:
  0.0 71.5 jit_solution(15011568769959635423)
XLA Ops:
  0.0 69.9 %shard_map.28 = f32[16,16,128]{2,1,0:T(8,128)} custom-call(f32[16,16,128]{2,1,0:T(8,128)} %refs_0_.1, f32[16,16,128]{2,1,0:T(8,128)} %refs_1_.1), custom_call_target="tpu_custom_call" | custom-call | tf_op jit(solution)/shard_map/pallas_call | solution.py:722
  69.9 1.6 %copy.4 = f32[16,16,128]{2,1,0:T(8,128)} copy(f32[16,16,128]{2,1,0:T(8,128)} %shard_map.28) | data formatting | bytes 262144

commit v5 on v4

--- a/solution.py
+++ b/solution.py
@@ -47,14 +47,12 @@
 
 def mml(m, v):
     m = m.astype(jnp.bfloat16)
-    high, mid, low = parts_of(v)
-    return dot(m, high) + (dot(m, mid) + dot(m, low))
+    return dot(jnp.concatenate([m, m, m], axis=1), jnp.concatenate(parts_of(v), axis=0))
 
 
 def mmr(v, m):
     m = m.astype(jnp.bfloat16)
-    high, mid, low = parts_of(v)
-    return dot(high, m) + (dot(mid, m) + dot(low, m))
+    return dot(jnp.concatenate(parts_of(v), axis=1), jnp.concatenate([m, m, m], axis=0))
 
 
 def iota(shape, dim):

time: 71.6 us -> 70.8 us (0.989)
  Pallas kernels: 69.9 us -> 69 us
    pallas_call x1, Pallas kernels: 69.9 us -> 69 us  [local(): pl.pallas_call(functools.partial(kernel, sizes, names), out_shape=jax.Sha...]
where the time goes in v5:
time: 70.8 us; the launch traced here: 70.6 us
  Pallas kernels  69 us (97%)
  local copies, waits for them, and re-layouts  1.57 us (2%)
    pallas_call x1, Pallas kernels, local(): pl.pallas_call(functools.partial(kernel, sizes, names), out_shape=jax.Sha...  69 us
    unnamed x1, local copies, waits for them, and re-layouts  1.57 us

profile of v5, /device:TPU:1, one launch (start us, length us, event | category | flops | bytes accessed | tf_op | source)
XLA Modules:
  0.0 70.6 jit_solution(13617124647426517517)
XLA Ops:
  0.0 69.0 %shard_map.28 = f32[16,16,128]{2,1,0:T(8,128)} custom-call(f32[16,16,128]{2,1,0:T(8,128)} %refs_0_.1, f32[16,16,128]{2,1,0:T(8,128)} %refs_1_.1), custom_call_target="tpu_custom_call" | custom-call | tf_op jit(solution)/shard_map/pallas_call | solution.py:720
  69.0 1.6 %copy.4 = f32[16,16,128]{2,1,0:T(8,128)} copy(f32[16,16,128]{2,1,0:T(8,128)} %shard_map.28) | data formatting | bytes 262144

commit v6 on v5

--- a/solution.py
+++ b/solution.py
@@ -16,7 +16,7 @@
 H0, H0R = 5, 3
 H1K, H1F, H1R = 6, 4, 5
 
-G0, G1, G2, G3 = 8, 20, 20, 32
+G0, G1, G2, G3 = 10, 20, 20, 32
 OWN0 = (slice(8, 24), slice(0, 128))
 
 

time: 70.8 us -> 69.8 us (0.986)
  Pallas kernels: 69 us -> 68.1 us
    pallas_call x1, Pallas kernels: 69 us -> 68.1 us  [local(): pl.pallas_call(functools.partial(kernel, sizes, names), out_shape=jax.Sha...]
where the time goes in v6:
time: 69.8 us; the launch traced here: 69.6 us
  Pallas kernels  68.1 us (98%)
  local copies, waits for them, and re-layouts  1.57 us (2%)
    pallas_call x1, Pallas kernels, local(): pl.pallas_call(functools.partial(kernel, sizes, names), out_shape=jax.Sha...  68.1 us
    unnamed x1, local copies, waits for them, and re-layouts  1.57 us

profile of v6, /device:TPU:1, one launch (start us, length us, event | category | flops | bytes accessed | tf_op | source)
XLA Modules:
  0.0 69.6 jit_solution(9640963715201033866)
XLA Ops:
  0.0 68.1 %shard_map.28 = f32[16,16,128]{2,1,0:T(8,128)} custom-call(f32[16,16,128]{2,1,0:T(8,128)} %refs_0_.1, f32[16,16,128]{2,1,0:T(8,128)} %refs_1_.1), custom_call_target="tpu_custom_call" | custom-call | tf_op jit(solution)/shard_map/pallas_call | solution.py:720
  68.1 1.6 %copy.4 = f32[16,16,128]{2,1,0:T(8,128)} copy(f32[16,16,128]{2,1,0:T(8,128)} %shard_map.28) | data formatting | bytes 262144
